TPU v7x, 32 devices: a whole 2x2x4 slice. The times are simulated.
32 devices in a mesh: groups: 2 (over y), pencil: 4 (over x, core), point: 4 (over z).
Axes of the slice: x: 2, y: 2, z: 4, core: 2. Of those that a mesh axis runs over, the one named last changes fastest.
Arguments:
- point_features: bfloat16 [64, 262144], P(None, ('groups', 'pencil', 'point')), parts along dimension 1, may hold values from -6 to 6
- point_position: float32 [3, 262144], P(None, ('groups', 'pencil', 'point')), parts along dimension 1, may hold values from 0 to 1
- block_counts: int32 [32, 64], P(('groups', 'pencil', 'point')), parts along dimension 0, may hold values from 1 to 3, 128 in all within a row
- pair_tile: int32 [4096], P(('groups', 'pencil', 'point')), parts along dimension 0, may hold values from 0 to 4095, as said below
- pair_offset: float32 [3, 4096], P(None, ('groups', 'pencil', 'point')), parts along dimension 1, may hold values from -1 to 1
- skip_weight: bfloat16 [64, 64], replicated, may hold values from -0.75 to 0.75
- spectral_weight: bfloat16 [64, 32, 64, 128], P('pencil'), may hold values from -2.09375 to 2.09375
Outputs:
- encoded: bfloat16 [512, 256, 2048], P(('groups', 'pencil'), None, 'point'), parts along dimension 0
There are 2 independent parts, one for each index of `groups`. A program takes and returns all parts, laid end to end along the dimension named above; an argument that names none is the same for every part. Nothing has to cross between parts.
Inputs may be any that keep to these rules, and one draw needn't show every extreme that they name: pair_tile // 1024 is the point index of the tile's owner in the same pencil row. The pairs of one device name tiles of one owner at most 32 times; in every pencil row some owner is named exactly 32 times by every device of that row. `block_counts`: the counts of one device sum to 128; a device's pairs are listed block by block, block 0 first.
All inputs are finite; a program needn't handle non-finite values.
Results may differ from a plain program's by a relative error of at most 0.005.
Values may be sent and summed in bfloat16 or wider, within the bound.
A program may use at most 256 MiB of HBM per device.

v0:
```python
import math

import jax
import jax.numpy as jnp
from jax import lax
from jax.sharding import PartitionSpec as P

NX = 256
NY = 256
MODES = 32
BLOCK = 128
TILE_CELLS = 128
ZL = 8
KMODES = 64
CAP = 32


def kernel_weights(spot_rows, offsets, tile_width, tile_height):
    cell_index = jnp.arange(tile_width * tile_height, dtype=jnp.int32)
    cell_x = (cell_index // tile_height).astype(jnp.float32) + 0.5
    cell_y = (cell_index % tile_height).astype(jnp.float32) + 0.5
    point_x = spot_rows[0] * float(tile_width) + offsets[0][:, None]
    point_y = spot_rows[1] * float(tile_height) + offsets[1][:, None]
    point_z = spot_rows[2] - 0.5 + offsets[2][:, None]
    gap_x = point_x[:, None, :] - cell_x[None, :, None]
    gap_y = point_y[:, None, :] - cell_y[None, :, None]
    distance = gap_x * gap_x + gap_y * gap_y + (point_z * point_z)[:, None, :]
    return jnp.exp(-distance).astype(jnp.bfloat16)


def wave_table(freqs, length, count):
    phase = freqs[:, None] * jnp.arange(count, dtype=jnp.int32)[None, :] % length
    angle = phase.astype(jnp.float32) * (2.0 * math.pi / length)
    return (jnp.cos(angle), jnp.sin(angle))


def einsum_high(form, left, right):
    return jnp.einsum(form, left, right, precision=lax.Precision.HIGHEST)


def mix_modes(modes, weight, form, channels):
    shape = modes.shape
    split_modes = modes.reshape(shape[0], shape[1], shape[2], shape[3] // channels, channels)
    real_part = einsum_high(form, split_modes[0], weight)
    imag_part = einsum_high(form, split_modes[1], weight)
    out_real = real_part[..., :channels] - imag_part[..., channels:]
    out_imag = real_part[..., channels:] + imag_part[..., :channels]
    return jnp.stack([out_real, out_imag]).reshape(shape)


def per_device(
    point_features,
    point_position,
    block_counts,
    pair_tile,
    pair_offset,
    skip_weight,
    spectral_weight,
):
    pencils = lax.axis_size("pencil")
    owners = lax.axis_size("point")
    channels = skip_weight.shape[0]
    tile_width = NX // pencils
    tile_height = TILE_CELLS // tile_width
    row_blocks = NY // tile_height
    tiles_dev = ZL * row_blocks
    blocks_dev = block_counts.shape[1]
    pairs_dev = pair_tile.shape[0]
    block_ends = jnp.cumsum(block_counts[0])
    pair_order = jnp.arange(pairs_dev, dtype=jnp.int32)
    block_of = jnp.sum((block_ends[None, :] <= pair_order[:, None]).astype(jnp.int32), axis=1)
    chosen_rows = jnp.take(point_features.reshape(channels, blocks_dev, BLOCK), block_of, axis=1)
    spot_rows = jnp.take(point_position.reshape(3, blocks_dev, BLOCK), block_of, axis=1)
    weights = kernel_weights(spot_rows, pair_offset, tile_width, tile_height)
    terms = jnp.einsum(
        "cpj,pkj->pck", chosen_rows, weights, preferred_element_type=jnp.float32
    ).astype(jnp.bfloat16)
    owner_index = pair_tile // tiles_dev
    tile_local = pair_tile % tiles_dev
    owner_picks = (owner_index[:, None] == jnp.arange(owners, dtype=jnp.int32)[None, :]).astype(
        jnp.int32
    )
    before = jnp.cumsum(owner_picks, axis=0) - owner_picks
    slot_index = jnp.sum(before * owner_picks, axis=1)
    outgoing = (
        jnp.zeros((owners, CAP, channels, TILE_CELLS), jnp.bfloat16)
        .at[owner_index, slot_index]
        .set(terms)
    )
    labels = jnp.full((owners, CAP), -1, jnp.int32).at[owner_index, slot_index].set(tile_local)
    arrived, arrived_labels = (
        lax.all_to_all(outgoing, "point", split_axis=0, concat_axis=0, tiled=True),
        lax.all_to_all(labels, "point", split_axis=0, concat_axis=0, tiled=True),
    )
    member = (
        arrived_labels.reshape(-1)[None, :] == jnp.arange(tiles_dev, dtype=jnp.int32)[:, None]
    ).astype(jnp.bfloat16)
    tile_sums = jnp.dot(
        member,
        arrived.reshape(owners * CAP, channels * TILE_CELLS),
        preferred_element_type=jnp.float32,
    )
    grid_tiles = tile_sums.astype(jnp.bfloat16).reshape(
        ZL, row_blocks, channels, tile_width, tile_height
    )
    latent = grid_tiles.transpose(3, 1, 4, 0, 2).reshape(tile_width, NY, ZL * channels)
    skip_term = jnp.einsum(
        "xyzi,io->xyzo",
        latent.reshape(tile_width, NY, ZL, channels),
        skip_weight,
        preferred_element_type=jnp.float32,
    )
    skip_term = skip_term.reshape(tile_width, NY, ZL * channels)
    x_index = jnp.arange(KMODES, dtype=jnp.int32)
    x_freqs = jnp.where(x_index < MODES, x_index, NX - KMODES + x_index)
    x_cosine, x_sine = wave_table(x_freqs, NX, NX)
    y_cosine, y_sine = wave_table(jnp.arange(MODES, dtype=jnp.int32), NY, NY)
    y_weight = jnp.where(jnp.arange(MODES) == 0, 1.0, 2.0).astype(jnp.float32)[:, None] / NY
    y_cos_back = y_cosine * y_weight
    y_sin_back = y_sine * y_weight
    mode_weight = spectral_weight.astype(jnp.float32)
    values = latent.astype(jnp.float32)
    y_modes = jnp.stack(
        [einsum_high("my,xyn->mxn", y_cosine, values), -einsum_high("my,xyn->mxn", y_sine, values)]
    )
    data = lax.all_to_all(y_modes, "pencil", split_axis=1, concat_axis=2, tiled=True)
    real_out = einsum_high("kx,mxn->mkn", x_cosine, data[0]) + einsum_high(
        "kx,mxn->mkn", x_sine, data[1]
    )
    imag_out = einsum_high("kx,mxn->mkn", x_cosine, data[1]) - einsum_high(
        "kx,mxn->mkn", x_sine, data[0]
    )
    both_modes = jnp.stack([real_out, imag_out])
    spectrum = lax.all_to_all(both_modes, "pencil", split_axis=2, concat_axis=1, tiled=True)
    mixed = mix_modes(spectrum, mode_weight, "mkzi,kmio->mkzo", channels)
    returned = lax.all_to_all(mixed, "pencil", split_axis=1, concat_axis=2, tiled=True)
    back_real = (
        einsum_high("kx,mkn->mxn", x_cosine, returned[0])
        - einsum_high("kx,mkn->mxn", x_sine, returned[1])
    ) / NX
    back_imag = (
        einsum_high("kx,mkn->mxn", x_cosine, returned[1])
        + einsum_high("kx,mkn->mxn", x_sine, returned[0])
    ) / NX
    data = lax.all_to_all(
        jnp.stack([back_real, back_imag]), "pencil", split_axis=2, concat_axis=1, tiled=True
    )
    wave = einsum_high("my,mxn->xyn", y_cos_back, data[0]) - einsum_high(
        "my,mxn->xyn", y_sin_back, data[1]
    )
    return jax.nn.gelu(wave + skip_term, approximate=False).astype(jnp.bfloat16)


def solution(mesh):
    placed = (
        P(None, ("groups", "pencil", "point")),
        P(None, ("groups", "pencil", "point")),
        P(("groups", "pencil", "point"), None),
        P(("groups", "pencil", "point")),
        P(None, ("groups", "pencil", "point")),
        P(),
        P("pencil", None, None, None),
    )
    return jax.shard_map(
        per_device,
        mesh=mesh,
        in_specs=placed,
        out_specs=P(("groups", "pencil"), None, "point"),
        check_vma=False,
    )
```

profile of v0, /device:TPU:0, one launch (start us, length us, event | category | flops | bytes accessed | tf_op | source)
XLA Modules:
  0.0 797.5 jit_solution(3052360433450509211)
XLA Ops:
  0.0 0.8 and_select_fusion.2
  1.2 0.6 broadcast_in_dim.32
  1.8 19.8 %scatter_fusion = s32[4,32]{1,0:T(4,128)} fusion(s32[4,32]{1,0:T(4,128)} %broadcast_in_dim.32, s32[128]{0:T(128)S(1)} %fusion.97, s32[128]{0:T(128)S(1)} %get-tuple-element.21), kind=kCustom, calls=%fused_computation.2 | custom fusion | bytes 2560 | tf_op jit(solution)/shard_map/scatter | solution.py:90
  21.6 6.3 all-to-all-start
  28.0 0.7 copy.80
  29.1 1.7 gather_fusion.1
  30.7 0.2 select_bitcast_fusion
  31.1 0.8 slice_bitcast_fusion.2
  31.9 0.3 copy_bitcast_fusion.3
  32.2 2.1 gather_fusion
  34.5 4.9 fusion.32
  39.5 1.8 broadcast_in_dim.36
  41.3 17.2 %scatter_fusion.1 = bf16[4,32,64,128]{3,2,1,0:T(8,128)(2,1)} fusion(bf16[4,32,64,128]{3,2,1,0:T(8,128)(2,1)} %broadcast_in_dim.36, s32[128]{0:T(128)S(1)} %fusion.97, bf16[128,64,128]{2,1,0:T(8,128)(2,1)S(1)} %fusion.32), kind=kCustom, calls=%fused_computation.3 | custom fusion | bytes 6292480 | tf_op jit(solution)/shard_map/scatter | solution.py:88
  58.5 5.4 all-to-all-start.1
  63.9 0.5 broadcast.355
  64.4 0.6 reduce.4
  65.0 46.5 %all-to-all-done.1 = bf16[4,32,64,128]{3,2,1,0:T(8,128)(2,1)S(1)} async-done(((bf16[4,32,64,128]{3,2,1,0:T(8,128)(2,1)}), bf16[4,32,64,128]{3,2,1,0:T(8,128)(2,1)S(1)}, u32[]{:S(2)}, u32[]{:S(2)}) %all-to-all-start.1) | async-done | bytes 2097184 | tf_op jit(solution)/shard_map/all_to_all | solution.py:92
  111.5 9.2 %convolution_convert_fusion = bf16[1024,8192]{1,0:T(8,128)(2,1)} fusion(bf16[16,8,64,128]{3,2,1,0:T(8,128)(2,1)S(1)} %bitcast.187, s32[128]{0:T(128)S(1)} %eq.50), kind=kOutput, calls=%fused_computation.26 | convolution fusion | flops 2156003328 | bytes 18874880 | tf_op jit(solution)/shard_map/dot_general | solution.py:98
  120.7 22.4 %copy.82 = bf16[1024,8192]{0,1:T(8,128)(2,1)} copy(bf16[1024,8192]{1,0:T(8,128)(2,1)} %convolution_convert_fusion) | data formatting | bytes 33554432 | tf_op jit(solution)/shard_map/convert_element_type | solution.py:103
  143.1 15.6 %copy.105 = bf16[1024,8,8,128]{3,2,1,0:T(8,128)(2,1)} copy(bf16[1024,8,8,128]{3,1,2,0:T(8,128)(2,1)} %bitcast.174) | data formatting | bytes 33554432
  158.7 45.4 %copy.83 = bf16[64,128,2,8,64]{4,3,2,1,0:T(8,128)(2,1)} copy(bf16[64,128,2,8,64]{1,3,2,0,4:T(8,128)(2,1)} %bitcast.173) | data formatting | bytes 33554432 | tf_op jit(solution)/shard_map/transpose | solution.py:106
  204.1 43.7 %reshape.215 = bf16[64,256,512]{2,1,0:T(8,128)(2,1)} reshape(bf16[64,128,2,8,64]{4,3,2,1,0:T(8,128)(2,1)} %copy.83) | data formatting | bytes 33554432 | tf_op jit(solution)/shard_map/reshape | solution.py:106
  247.8 12.9 %negate_bitcast_fusion = f32[1,32,64,512]{3,1,2,0:T(8,128)S(1)} fusion(bf16[64,256,512]{2,1,0:T(8,128)(2,1)} %reshape.215), kind=kOutput, calls=%fused_computation.43 | convolution fusion | flops 3222388736 | bytes 20971520 | tf_op jit(solution)/shard_map/my,xyn->mxn/dot_general | solution.py:38
  260.7 8.7 %convolution_bitcast_fusion = f32[1,32,64,512]{3,1,2,0:T(8,128)S(1)} fusion(bf16[64,256,512]{2,1,0:T(8,128)(2,1)S(1)} %copy-done.2), kind=kOutput, calls=%fused_computation.49 | convolution fusion | flops 3221340160 | bytes 20971520 | tf_op jit(solution)/shard_map/my,xyn->mxn/dot_general | solution.py:38
  269.4 1.9 pad_maximum_fusion
  271.3 8.3 %copy.84 = f32[2,32,64,512]{3,2,0,1:T(8,128)} copy(f32[2,32,64,512]{3,1,2,0:T(8,128)S(1)} %pad_maximum_fusion) | data formatting | bytes 16777216 | tf_op jit(solution)/shard_map/stack | solution.py:123
  279.5 5.8 all-to-all-start.2
  285.4 93.0 %all-to-all-done.2 = f32[2,32,64,512]{3,2,0,1:T(8,128)} async-done(((f32[2,32,64,512]{3,2,0,1:T(8,128)}), f32[2,32,64,512]{3,2,0,1:T(8,128)}, u32[]{:S(2)}, u32[]{:S(2)}) %all-to-all-start.2) | async-done | bytes 8388640 | tf_op jit(solution)/shard_map/all_to_all | solution.py:126
  378.4 4.4 copy.129
  382.8 1.8 fusion.148
  384.6 3.1 fusion.50
  387.8 3.2 fusion.52
  390.9 3.2 fusion.35
  394.1 3.6 fusion.36
  397.8 0.2 pad_maximum_fusion.2
  398.0 1.2 copy.86
  399.2 28.2 %all_to_all.74 = f32[2,8,64,512]{3,1,0,2:T(8,128)S(1)} all-to-all(f32[2,8,64,512]{3,1,0,2:T(8,128)S(1)} %copy.86), channel_id=1, replica_groups=mesh['groups'=2,'pencil'=4,'point'=4] {'pencil'}, dimensions={2} | all-to-all | bytes 4194304 | tf_op jit(solution)/shard_map/all_to_all | solution.py:134
  427.4 1.2 copy.131
  428.6 1.2 fusion.150
  429.8 1.6 squeeze.35
  431.4 1.7 squeeze.34
  433.1 9.1 %fusion.12 = f32[32,16,8,128]{3,2,1,0:T(8,128)S(1)} fusion(f32[32,16,8,64]{3,2,1,0:T(8,128)S(1)} %squeeze.35, bf16[16,32,64,128]{3,2,1,0:T(8,128)(2,1)} %param.13), kind=kOutput, calls=%fused_computation.31 | convolution fusion | flops 402653184 | bytes 11534336 | tf_op jit(solution)/shard_map/mkzi,kmio->mkzo/dot_general | solution.py:38
  442.2 9.0 %fusion.14 = f32[32,16,8,128]{3,2,1,0:T(8,128)S(1)} fusion(f32[32,16,8,64]{3,2,1,0:T(8,128)S(1)} %copy-done.3, bf16[16,32,64,128]{3,2,1,0:T(8,128)(2,1)} %param.13), kind=kOutput, calls=%fused_computation.33 | convolution fusion | flops 402653184 | bytes 11534336 | tf_op jit(solution)/shard_map/mkzi,kmio->mkzo/dot_general | solution.py:38
  451.2 2.5 slice_subtract_fusion
  453.6 1.9 stack.43
  455.6 1.5 stack.42
  457.0 1.5 pad_maximum_fusion.3
  458.5 28.2 %all_to_all.75 = f32[2,32,16,512]{3,2,0,1:T(8,128)S(1)} all-to-all(f32[2,32,16,512]{3,2,0,1:T(8,128)S(1)} %pad_maximum_fusion.3), channel_id=1, replica_groups=mesh['groups'=2,'pencil'=4,'point'=4] {'pencil'}, dimensions={1} | all-to-all | bytes 4194304 | tf_op jit(solution)/shard_map/all_to_all | solution.py:136
  486.7 0.3 copy.130
  487.0 0.2 fusion.149
  487.2 3.8 fusion.46
  491.0 3.8 fusion.48
  494.9 4.0 multiply_bitcast_fusion
  498.9 4.2 multiply_bitcast_fusion.1
  503.1 4.0 pad_maximum_fusion.1
  507.1 10.5 %copy.93 = f32[2,8,256,512]{3,1,0,2:T(8,128)} copy(f32[2,8,256,512]{2,3,1,0:T(8,128)} %pad_maximum_fusion.1) | data formatting | bytes 16777216 | tf_op jit(solution)/shard_map/stack | solution.py:146
  517.5 5.8 all-to-all-start.5
  523.5 28.7 %fusion.3 = f32[64,256,8,64]{1,3,2,0:T(8,128)} fusion(bf16[64,256,8,64]{3,2,1,0:T(8,128)(2,1)} %bitcast.172, bf16[64,64]{1,0:T(8,128)(2,1)S(1)} %copy-done.4), kind=kOutput, calls=%fused_computation.9 | convolution fusion | flops 1073741824 | bytes 50339840 | tf_op jit(solution)/shard_map/xyzi,io->xyzo/dot_general | solution.py:107
  552.2 64.3 %all-to-all-done.5 = f32[2,8,256,512]{3,1,0,2:T(8,128)} async-done(((f32[2,8,256,512]{3,1,0,2:T(8,128)}), f32[2,8,256,512]{3,1,0,2:T(8,128)}, u32[]{:S(2)}, u32[]{:S(2)}) %all-to-all-start.5) | async-done | bytes 8388640 | tf_op jit(solution)/shard_map/all_to_all | solution.py:145
  616.5 11.6 %copy.94 = f32[2,8,256,512]{3,2,1,0:T(8,128)} copy(f32[2,8,256,512]{3,1,0,2:T(8,128)} %all-to-all-done.5) | data formatting | bytes 16777216 | tf_op jit(solution)/shard_map/all_to_all | solution.py:145
  628.1 8.9 %fusion.147 = (f32[1,4,8,64,512]{4,3,1,2,0:T(8,128)}, f32[1,4,8,64,512]{4,3,1,2,0:T(8,128)}) fusion(f32[2,4,8,64,512]{4,3,1,2,0:T(8,128)} %bitcast.182), kind=kLoop, calls=%fused_computation.207 | loop fusion | bytes 16777216 | tf_op jit(solution)/shard_map/slice | solution.py:149
  637.1 32.3 %fusion.18 = f32[64,512,256]{2,1,0:T(8,128)} fusion(f32[1,4,8,64,512]{4,3,1,2,0:T(8,128)} %get-tuple-element.6, f32[32]{0:T(128)S(1)} %fusion.94), kind=kOutput, calls=%fused_computation.37 | convolution fusion | flops 3221348352 | bytes 37748864 | tf_op jit(solution)/shard_map/my,mxn->xyn/dot_general | solution.py:38
  669.4 105.4 %fusion.2 = bf16[64,256,512]{1,2,0:T(8,128)(2,1)} fusion(f32[64,256,8,64]{1,3,2,0:T(8,128)S(1)} %bitcast.176, f32[64,512,256]{2,1,0:T(8,128)} %fusion.18, f32[1,4,8,64,512]{4,3,1,2,0:T(8,128)} %get-tuple-element.5, f32[32,256,1]{1,0,2:T(8,128)S(1)} %fusion.167), kind=kOutput, calls=%fused_computation.7 | convolution fusion | flops 3783262208 | bytes 88113152 | tf_op jit(solution)/shard_map/my,mxn->xyn/dot_general | solution.py:38
  774.8 22.5 %copy.100 = bf16[64,256,512]{2,1,0:T(8,128)(2,1)} copy(bf16[64,256,512]{1,2,0:T(8,128)(2,1)} %fusion.2) | data formatting | bytes 33554432 | tf_op jit(solution)/shard_map/convert_element_type | solution.py:151
  (46 shorter events, 1.4 us)
Async XLA Ops:
  0.0 31.9 %copy-start = (bf16[64,8192]{1,0:T(8,128)(2,1)S(1)}, bf16[64,8192]{1,0:T(8,128)(2,1)}, u32[]{:S(2)}) copy-start(bf16[64,8192]{1,0:T(8,128)(2,1)} %param.7) | copy-start | bytes 3145732
  21.6 36.9 %all-to-all-start = ((s32[4,1,32]{2,1,0:T(1,128)}), s32[4,1,32]{2,1,0:T(1,128)S(1)}, u32[]{:S(2)}, u32[]{:S(2)}) async-start(s32[4,1,32]{2,1,0:T(1,128)} %bitcast.5), calls=%async_computation | async-start | bytes 4096 | tf_op jit(solution)/shard_map/all_to_all | solution.py:93
  58.5 53.0 %all-to-all-start.1 = ((bf16[4,32,64,128]{3,2,1,0:T(8,128)(2,1)}), bf16[4,32,64,128]{3,2,1,0:T(8,128)(2,1)S(1)}, u32[]{:S(2)}, u32[]{:S(2)}) async-start(bf16[4,32,64,128]{3,2,1,0:T(8,128)(2,1)} %scatter_fusion.1), calls=%async_computation.1 | async-start | bytes 4194304 | tf_op jit(solution)/shard_map/all_to_all | solution.py:92
  247.8 12.9 %copy-start.2 = (bf16[64,256,512]{2,1,0:T(8,128)(2,1)S(1)}, bf16[64,256,512]{2,1,0:T(8,128)(2,1)}, u32[]{:S(2)}) copy-start(bf16[64,256,512]{2,1,0:T(8,128)(2,1)} %reshape.215) | copy-start | bytes 50331652
  279.5 98.8 %all-to-all-start.2 = ((f32[2,32,64,512]{3,2,0,1:T(8,128)}), f32[2,32,64,512]{3,2,0,1:T(8,128)}, u32[]{:S(2)}, u32[]{:S(2)}) async-start(f32[2,32,64,512]{3,2,0,1:T(8,128)} %copy.84), calls=%async_computation.2 | async-start | bytes 16777216 | tf_op jit(solution)/shard_map/all_to_all | solution.py:126
  433.1 9.1 %copy-start.3 = (f32[32,16,8,64]{3,2,1,0:T(8,128)S(1)}, f32[32,16,8,64]{3,2,1,0:T(8,128)}, u32[]{:S(2)}) copy-start(f32[32,16,8,64]{3,2,1,0:T(8,128)} %squeeze.34) | copy-start | bytes 3145732
  517.5 6.0 copy-start.4
  517.5 99.0 %all-to-all-start.5 = ((f32[2,8,256,512]{3,1,0,2:T(8,128)}), f32[2,8,256,512]{3,1,0,2:T(8,128)}, u32[]{:S(2)}, u32[]{:S(2)}) async-start(f32[2,8,256,512]{3,1,0,2:T(8,128)} %copy.93), calls=%async_computation.5 | async-start | bytes 16777216 | tf_op jit(solution)/shard_map/all_to_all | solution.py:145
  628.1 41.2 %slice-start = ((s8[33554432]{0:T(1024)(128)(4,1)}), s8[4194304]{0:T(1024)(128)(4,1)S(1)}, s32[]{:S(2)}) async-start(s8[33554432]{0:T(1024)(128)(4,1)} %bitcast.175), calls=%async_computation.6 | async-start | bytes 8388608
  628.1 41.2 %slice-start.1 = ((s8[33554432]{0:T(1024)(128)(4,1)}), s8[4194304]{0:T(1024)(128)(4,1)S(1)}, s32[]{:S(2)}) async-start(s8[33554432]{0:T(1024)(128)(4,1)} %bitcast.175), calls=%async_computation.7 | async-start | bytes 8388608
  628.1 41.2 %slice-start.2 = ((s8[33554432]{0:T(1024)(128)(4,1)}), s8[4194304]{0:T(1024)(128)(4,1)S(1)}, s32[]{:S(2)}) async-start(s8[33554432]{0:T(1024)(128)(4,1)} %bitcast.175), calls=%async_computation.8 | async-start | bytes 8388608
  637.0 32.3 %slice-start.3 = ((s8[33554432]{0:T(1024)(128)(4,1)}), s8[4194304]{0:T(1024)(128)(4,1)S(1)}, s32[]{:S(2)}) async-start(s8[33554432]{0:T(1024)(128)(4,1)} %bitcast.175), calls=%async_computation.9 | async-start | bytes 8388608
  637.0 32.3 %slice-start.4 = ((s8[33554432]{0:T(1024)(128)(4,1)}), s8[4194304]{0:T(1024)(128)(4,1)S(1)}, s32[]{:S(2)}) async-start(s8[33554432]{0:T(1024)(128)(4,1)} %bitcast.175), calls=%async_computation.10 | async-start | bytes 8388608
  637.0 32.3 %slice-start.5 = ((s8[33554432]{0:T(1024)(128)(4,1)}), s8[4194304]{0:T(1024)(128)(4,1)S(1)}, s32[]{:S(2)}) async-start(s8[33554432]{0:T(1024)(128)(4,1)} %bitcast.175), calls=%async_computation.11 | async-start | bytes 8388608
  637.0 32.3 %slice-start.6 = ((s8[33554432]{0:T(1024)(128)(4,1)}), s8[4194304]{0:T(1024)(128)(4,1)S(1)}, s32[]{:S(2)}) async-start(s8[33554432]{0:T(1024)(128)(4,1)} %bitcast.175), calls=%async_computation.12 | async-start | bytes 8388608
  637.0 32.3 %slice-start.7 = ((s8[33554432]{0:T(1024)(128)(4,1)}), s8[4194304]{0:T(1024)(128)(4,1)S(1)}, s32[]{:S(2)}) async-start(s8[33554432]{0:T(1024)(128)(4,1)} %bitcast.175), calls=%async_computation.13 | async-start | bytes 8388608
  774.8 22.5 %copy-start.1 = (bf16[64,8192]{1,0:T(8,128)(2,1)S(1)}, bf16[64,8192]{1,0:T(8,128)(2,1)}, u32[]{:S(2)}) copy-start(bf16[64,8192]{1,0:T(8,128)(2,1)} %param.7) | copy-start | bytes 3145732
where the time goes:
time: 808 us; the launch traced here: 797 us
  local copies, waits for them, and re-layouts  252 us (31%)
  matrix products  249 us (31%)
  waiting for transfers between devices  204 us (25%)
  blocking collectives  56.3 us (7%)
  starting transfers between devices  23.3 us (3%)
  other arithmetic  12.7 us (2%)
    dot_general x14, matrix products, einsum_high(): return jnp.einsum(form, left, right, precision=lax.Precision.HIGHEST)  206 us
    all_to_all x1, waiting for transfers between devices, per_device(): lax.all_to_all(y_modes, 'pencil', split_axis=1, concat_axis=2, tiled=True)  93 us
    all_to_all x1, waiting for transfers between devices, per_device(): lax.all_to_all(jnp.stack([back_real, back_imag]), 'pencil', split_axis=2,...  64.3 us
    all_to_all x1, waiting for transfers between devices, per_device(): lax.all_to_all(outgoing, 'point', split_axis=0, concat_axis=0, tiled=True)  46.5 us
    transpose x1, local copies, waits for them, and re-layouts, per_device(): grid_tiles.transpose(3, 1, 4, 0, 2).reshape(tile_width, NY, ZL * channels)  45.4 us
    reshape x1, local copies, waits for them, and re-layouts, per_device(): grid_tiles.transpose(3, 1, 4, 0, 2).reshape(tile_width, NY, ZL * channels)  43.7 us
    dot_general x1, matrix products, per_device(): jnp.einsum('xyzi,io->xyzo', latent.reshape(tile_width, NY, ZL, channels),...  28.7 us
    all_to_all x1, blocking collectives, per_device(): lax.all_to_all(mixed, 'pencil', split_axis=1, concat_axis=2, tiled=True)  28.2 us
  transfers between devices with their start and end apart: 4, of which 3 were waited for; matrix products, arithmetic and copies ran while one was open for 8% of the time, Pallas kernels for 0%

commit v1 on v0

v1 whole, which is shorter than its diff:
```python
import functools
import math

import jax
import jax.numpy as jnp
from jax import lax
from jax.experimental import pallas as pl
from jax.experimental.pallas import tpu as pltpu
from jax.sharding import PartitionSpec as P

NX = 256
NY = 256
MODES = 32
BLOCK = 128
TILE_CELLS = 128
ZL = 8
KMODES = 64
CAP = 32
HALF_Z = ZL // 2
LANES = 128
VMEM_LIMIT = 56 * 1024 * 1024


def dot(left, right):
    return jnp.dot(left, right, preferred_element_type=jnp.float32)


def terms_kernel(tiles_dev, counts, tiles, offsets, features, position, out, used):
    slots, width, lanes = out.shape
    channels = features.shape[0]
    height = lanes // channels
    owners = slots // CAP
    pairs = tiles.shape[0]
    for owner in range(owners):
        used[owner] = 0
    out[...] = jnp.zeros_like(out)
    cell_x = lax.broadcasted_iota(jnp.int32, (width, BLOCK), 0).astype(jnp.float32) + 0.5

    def one(pair, carry):
        block, end = carry
        moved = (pair >= end).astype(jnp.int32)
        block = block + moved
        end = end + moved * counts[0, block]
        at = pl.ds(pl.multiple_of(block * BLOCK, BLOCK), BLOCK)
        spot = position[:, at]
        gap_x = spot[0:1] * float(width) + offsets[0, pair] - cell_x
        along_x = jnp.exp(-(gap_x * gap_x))
        point_y = spot[1:2] * float(height) + offsets[1, pair]
        point_z = spot[2:3] - 0.5 + offsets[2, pair]
        square_z = point_z * point_z
        rows = []
        for row in range(height):
            gap_y = point_y - (row + 0.5)
            rows.append((along_x * jnp.exp(-(gap_y * gap_y + square_z))).astype(jnp.bfloat16))
        cells = jnp.concatenate(rows, axis=0)
        term = lax.dot_general(
            cells, features[:, at], (((1,), (1,)), ((), ())), preferred_element_type=jnp.float32
        )
        term = jnp.concatenate(
            [term[row * width : (row + 1) * width] for row in range(height)], axis=1
        )
        owner = tiles[pair] // tiles_dev
        slot = used[owner]
        used[owner] = slot + 1
        out[owner * CAP + slot] = term.astype(jnp.bfloat16)
        return block, end

    lax.fori_loop(0, pairs, one, (jnp.int32(0), counts[0, 0]), unroll=4)


def make_terms(features, position, counts, tiles, offsets, owners, width, height, tiles_dev):
    channels = features.shape[0]
    smem = pl.BlockSpec(memory_space=pltpu.SMEM)
    vmem = pl.BlockSpec(memory_space=pltpu.VMEM)
    return pl.pallas_call(
        functools.partial(terms_kernel, tiles_dev),
        out_shape=jax.ShapeDtypeStruct((owners * CAP, width, height * channels), jnp.bfloat16),
        in_specs=[smem, smem, smem, vmem, vmem],
        out_specs=vmem,
        scratch_shapes=[pltpu.SMEM((owners,), jnp.int32)],
        compiler_params=pltpu.CompilerParams(vmem_limit_bytes=VMEM_LIMIT),
    )(counts, tiles, offsets, features, position)


def forward_kernel(height, arrived, x_wave, y_wave, out, held):
    slots, width, lanes = arrived.shape
    parts, _ = x_wave.shape[1:]
    steps = parts // 2
    rows = out.shape[1]
    channels = lanes // height
    groups = lanes // LANES

    def one(slot, carry):
        wave = dot(x_wave[0], arrived[slot])
        for group in range(groups):
            held[group, pl.ds(slot, parts, stride=slots), :] = wave[
                :, group * LANES : (group + 1) * LANES
            ]
        return carry

    lax.fori_loop(0, slots, one, 0, unroll=4)

    def mode(index, carry):
        both = [
            jnp.concatenate(
                [
                    held[
                        group,
                        pl.ds(pl.multiple_of((index + part * steps) * slots, slots), slots),
                        :,
                    ]
                    for part in range(2)
                ],
                axis=0,
            ).astype(jnp.bfloat16)
            for group in range(groups)
        ]
        real_sum = None
        for row in range(height):
            group, first = divmod(row * channels, LANES)
            piece = dot(y_wave[row], both[group][:, first : first + channels])
            real_sum = piece if real_sum is None else real_sum + piece
        out[index] = jnp.concatenate([real_sum[:rows], real_sum[rows:]], axis=1).astype(
            jnp.bfloat16
        )
        return carry

    lax.fori_loop(0, steps, mode, 0, unroll=2)


def forward(arrived, x_wave, y_wave, height, chunk):
    slots, width, lanes = arrived.shape
    channels = lanes // height
    rows = y_wave.shape[1] // 2
    steps = KMODES // chunk
    whole = lambda shape: pl.BlockSpec(shape, lambda step: (0,) * len(shape))
    return pl.pallas_call(
        functools.partial(forward_kernel, height),
        grid=(steps,),
        out_shape=jax.ShapeDtypeStruct((KMODES, rows, 2 * channels), jnp.bfloat16),
        in_specs=[
            whole(arrived.shape),
            pl.BlockSpec((1, 2 * chunk, width), lambda step: (step, 0, 0)),
            whole(y_wave.shape),
        ],
        out_specs=pl.BlockSpec((chunk, rows, 2 * channels), lambda step: (step, 0, 0)),
        scratch_shapes=[pltpu.VMEM((lanes // LANES, 2 * chunk * slots, LANES), jnp.float32)],
        compiler_params=pltpu.CompilerParams(vmem_limit_bytes=VMEM_LIMIT),
    )(arrived, x_wave, y_wave)


def mix_kernel(spectra, weight, out, held):
    sources, _, rows, lanes = spectra.shape
    count = pl.num_programs(0)
    step = pl.program_id(0)
    stride = held.shape[0] // rows
    channels = lanes // 2
    row = lax.broadcasted_iota(jnp.int32, (ZL, lanes), 0)
    lane = lax.broadcasted_iota(jnp.int32, (ZL, lanes), 1)
    keep = (row < HALF_Z) == (lane < channels)
    for mode in range(MODES):
        at = slice(mode * ZL, (mode + 1) * ZL)
        total = spectra[0, 0, at].astype(jnp.float32)
        for source in range(1, sources):
            total = total + spectra[source, 0, at].astype(jnp.float32)
        plain = weight[0, mode]
        turned = jnp.concatenate([-plain[:, channels:], plain[:, :channels]], axis=1)
        mixed = dot(total.astype(jnp.bfloat16), jnp.concatenate([plain, turned], axis=0))
        other = pltpu.roll(pltpu.roll(mixed, HALF_Z, 0), channels, 1)
        held[pl.ds(mode * ZL * stride + step, ZL, stride=stride), :] = jnp.where(
            keep, mixed, other
        )

    @pl.when(step == count - 1)
    def _():
        out[...] = held[...].reshape(out.shape).astype(jnp.bfloat16)


def mix(spectra, weight):
    sources, own, rows, lanes = spectra.shape
    return pl.pallas_call(
        mix_kernel,
        grid=(own,),
        out_shape=jax.ShapeDtypeStruct((rows, own, lanes), jnp.bfloat16),
        in_specs=[
            pl.BlockSpec((sources, 1, rows, lanes), lambda step: (0, step, 0, 0)),
            pl.BlockSpec((1,) + weight.shape[1:], lambda step: (step, 0, 0, 0)),
        ],
        out_specs=pl.BlockSpec((rows, own, lanes), lambda step: (0, 0, 0)),
        scratch_shapes=[pltpu.VMEM((rows * own, lanes), jnp.float32)],
        compiler_params=pltpu.CompilerParams(vmem_limit_bytes=VMEM_LIMIT),
    )(spectra, weight)


def backward_kernel(height, mixed, terms, x_back, y_back, layer_mask, skip, out, held):
    sources, rows, own, lanes = mixed.shape
    width = x_back.shape[0] // 2
    channels = lanes // 2
    per_step = out.shape[0]
    step = pl.program_id(0)

    @pl.when(step == 0)
    def _():
        def mode(index, carry):
            for layer in range(HALF_Z):
                modes = jnp.concatenate(
                    [
                        mixed[source, index * ZL + part * HALF_Z + layer]
                        for part in range(2)
                        for source in range(sources)
                    ],
                    axis=0,
                )
                held[layer, pl.ds(index, 2 * width, stride=MODES), :] = dot(x_back[...], modes)
            return carry

        lax.fori_loop(0, MODES, mode, 0, unroll=2)

    for inner in range(per_step):
        x = step * per_step + inner
        parts = [
            jnp.concatenate(
                [
                    held[
                        layer,
                        pl.ds(pl.multiple_of((part * width + x) * MODES, MODES), MODES),
                        :,
                    ]
                    for layer in range(HALF_Z)
                ],
                axis=1,
            ).astype(jnp.bfloat16)
            for part in range(2)
        ]
        skipped = dot(terms[inner], skip[...]).astype(jnp.bfloat16)
        for row in range(height):
            piece = skipped[:, row * channels : (row + 1) * channels]
            pair = jnp.concatenate([piece, piece], axis=1)
            parts.append(jnp.concatenate([pair] * HALF_Z, axis=1) * layer_mask[...])
        value = dot(y_back[...], jnp.concatenate(parts, axis=0))
        out[inner] = (0.5 * value * (1.0 + lax.erf(value * math.sqrt(0.5)))).astype(jnp.bfloat16)


def backward(mixed, terms, x_back, y_back, layer_mask, skip, height, per_step):
    width, slots, lanes = terms.shape
    whole = lambda shape: pl.BlockSpec(shape, lambda step: (0,) * len(shape))
    depth = layer_mask.shape[1]
    return pl.pallas_call(
        functools.partial(backward_kernel, height),
        grid=(width // per_step,),
        out_shape=jax.ShapeDtypeStruct((width, NY, depth), jnp.bfloat16),
        in_specs=[
            whole(mixed.shape),
            pl.BlockSpec((per_step, slots, lanes), lambda step: (step, 0, 0)),
            whole(x_back.shape),
            whole(y_back.shape),
            whole(layer_mask.shape),
            whole(skip.shape),
        ],
        out_specs=pl.BlockSpec((per_step, NY, depth), lambda step: (step, 0, 0)),
        scratch_shapes=[pltpu.VMEM((HALF_Z, 2 * width * MODES, mixed.shape[3]), jnp.float32)],
        compiler_params=pltpu.CompilerParams(vmem_limit_bytes=VMEM_LIMIT),
    )(mixed, terms, x_back, y_back, layer_mask, skip)


def angle(phase, length):
    return (phase % length).astype(jnp.float32) * (2.0 * math.pi / length)


def per_device(
    point_features,
    point_position,
    block_counts,
    pair_tile,
    pair_offset,
    skip_weight,
    spectral_weight,
):
    pencils = lax.axis_size("pencil")
    owners = lax.axis_size("point")
    pencil = lax.axis_index("pencil")
    me = lax.axis_index("point")
    channels = skip_weight.shape[0]
    width = NX // pencils
    height = TILE_CELLS // width
    row_blocks = NY // height
    tiles_dev = ZL * row_blocks
    slots = owners * CAP
    own = KMODES // pencils
    bf16 = jnp.bfloat16

    row_tiles = lax.all_gather(pair_tile, "point")
    terms = make_terms(
        point_features,
        point_position,
        block_counts,
        pair_tile,
        pair_offset,
        owners,
        width,
        height,
        tiles_dev,
    )
    arrived = lax.all_to_all(terms, "point", split_axis=0, concat_axis=0, tiled=True)

    mine = (row_tiles // tiles_dev == me).astype(jnp.int32)
    place = jnp.cumsum(mine, axis=1) - 1
    hit = (place[:, :, None] == jnp.arange(CAP, dtype=jnp.int32)) & (mine[:, :, None] == 1)
    labels = (
        jnp.sum(jnp.where(hit, (row_tiles % tiles_dev + 1)[:, :, None], 0), axis=1) - 1
    ).reshape(slots)
    layer_of = jnp.where(labels >= 0, labels // row_blocks, -1)
    block_of = labels % row_blocks

    modes = jnp.arange(MODES, dtype=jnp.int32)
    x_index = jnp.arange(KMODES, dtype=jnp.int32)
    x_freqs = jnp.where(x_index < MODES, x_index, NX - KMODES + x_index)
    x_cells = pencil * width + jnp.arange(width, dtype=jnp.int32)
    x_angle = angle(x_freqs[:, None] * x_cells[None, :], NX)
    x_cos, x_sin = jnp.cos(x_angle), jnp.sin(x_angle)
    chunk = KMODES if slots * height * channels * KMODES * 8 <= 16 * 1024 * 1024 else 8
    steps = KMODES // chunk
    x_wave = (
        jnp.stack([x_cos, -x_sin])
        .reshape(2, steps, chunk, width)
        .transpose(1, 0, 2, 3)
        .reshape(steps, 2 * chunk, width)
        .astype(bf16)
    )
    x_back = jnp.concatenate(
        [
            jnp.concatenate([x_cos.T, -x_sin.T], axis=1),
            jnp.concatenate([x_sin.T, x_cos.T], axis=1),
        ],
        axis=0,
    ).astype(bf16)

    pair_y = block_of[None, :] * height + jnp.arange(height, dtype=jnp.int32)[:, None]
    y_angle = angle(modes[None, :, None] * pair_y[:, None, :], NY)
    y_cos, y_sin = jnp.cos(y_angle).astype(bf16), jnp.sin(y_angle).astype(bf16)
    order = jnp.arange(ZL, dtype=jnp.int32)
    order = order % HALF_Z * 2 + order // HALF_Z
    layer_hit = layer_of[None, :] == order[:, None]
    turned = jnp.stack(
        [
            jnp.stack([y_cos, y_sin], axis=2),
            jnp.stack([-y_sin, y_cos], axis=2),
        ],
        axis=1,
    )
    y_wave = jnp.where(
        layer_hit[None, None, None, :, None, :], turned[:, :, :, None], jnp.zeros((), bf16)
    ).reshape(height, 2 * MODES * ZL, 2 * slots)

    rows_y = jnp.arange(NY, dtype=jnp.int32)
    back_angle = angle(rows_y[:, None] * modes[None, :], NY)
    scale = jnp.where(modes == 0, 1.0, 2.0).astype(jnp.float32)[None, :] / (NX * NY)
    y_back = jnp.concatenate(
        [
            (jnp.cos(back_angle) * scale).astype(bf16),
            (-jnp.sin(back_angle) * scale).astype(bf16),
            (rows_y[:, None] == pair_y.reshape(-1)[None, :]).astype(bf16),
        ],
        axis=1,
    )
    lane_layer = jnp.arange(ZL * channels, dtype=jnp.int32) // channels
    layer_mask = (layer_of[:, None] == lane_layer[None, :]).astype(bf16)
    skip = jnp.kron(jnp.eye(height, dtype=bf16), skip_weight)

    partial = forward(arrived, x_wave, y_wave, height, chunk)
    spectra = lax.all_to_all(partial, "pencil", split_axis=0, concat_axis=0, tiled=True)
    mixed = mix(spectra.reshape(pencils, own, MODES * ZL, 2 * channels), spectral_weight)
    gathered = lax.all_gather(mixed, "pencil")
    by_row = arrived.transpose(1, 0, 2)
    return backward(
        gathered, by_row, x_back, y_back, layer_mask, skip, height, 4 if width % 4 == 0 else 1
    )


def solution(mesh):
    placed = (
        P(None, ("groups", "pencil", "point")),
        P(None, ("groups", "pencil", "point")),
        P(("groups", "pencil", "point"), None),
        P(("groups", "pencil", "point")),
        P(None, ("groups", "pencil", "point")),
        P(),
        P("pencil", None, None, None),
    )
    return jax.shard_map(
        per_device,
        mesh=mesh,
        in_specs=placed,
        out_specs=P(("groups", "pencil"), None, "point"),
        check_vma=False,
    )
```

time: 808 us -> 261 us (0.32); the launches traced: 797 us -> 260 us
  matrix products: 249 us -> 0 us
  local copies, waits for them, and re-layouts: 252 us -> 5.09 us
  waiting for transfers between devices: 204 us -> 36.7 us
  Pallas kernels: 0 us -> 99 us
  blocking collectives: 56.3 us -> 93.6 us
  starting transfers between devices: 23.3 us -> 6.32 us
  between operations: 0.57 us -> 13.5 us
    dot_general x17 -> x0, matrix products: 249 us -> none  [the longest x14 206 us: einsum_high(): return jnp.einsum(form, left, right, precision=lax.Precision.HIGHEST)]
    all_to_all x4 -> x1, waiting for transfers between devices: 204 us -> 5.55 us  [per_device(): lax.all_to_all(terms, 'point', split_axis=0, concat_axis=0, tiled=True)]
    pallas_call x0 -> x4, Pallas kernels: none -> 99 us  [the longest x1 40.4 us: backward(): pl.pallas_call(functools.partial(backward_kernel, height), grid=(width //...]
    transpose x1 -> x0, local copies, waits for them, and re-layouts: 45.4 us -> none  [per_device(): grid_tiles.transpose(3, 1, 4, 0, 2).reshape(tile_width, NY, ZL * channels)]
    convert_element_type x2 -> x1, local copies, waits for them, and re-layouts: 44.9 us -> 0.1 us  [angle(): return (phase % length).astype(jnp.float32) * (2.0 * math.pi / length)]
    reshape x2 -> x0, local copies, waits for them, and re-layouts: 44 us -> none  [the longest x1 43.7 us: per_device(): grid_tiles.transpose(3, 1, 4, 0, 2).reshape(tile_width, NY, ZL * channels)]
    all_gather x0 -> x1, blocking collectives: none -> 39.7 us  [per_device(): row_tiles = lax.all_gather(pair_tile, 'point')]
    scatter x2 -> x0, local copies, waits for them, and re-layouts: 37 us -> none  [the longest x1 19.8 us: per_device(): jnp.full((owners, CAP), -1, jnp.int32).at[owner_index, slot_index]]
  transfers between devices with their start and end apart: 4 -> 2, of which waited for: 3 -> 2; matrix products, arithmetic and copies ran while one was open for 8% -> 4% of each run, Pallas kernels for 0% -> 0%
where the time goes in v1:
time: 261 us; the launch traced here: 260 us
  Pallas kernels  99 us (38%)
  blocking collectives  93.6 us (36%)
  waiting for transfers between devices  36.7 us (14%)
  between operations  13.5 us (5%)
  starting transfers between devices  6.32 us (2%)
  other arithmetic  5.74 us (2%)
  local copies, waits for them, and re-layouts  5.09 us (2%)
    all_to_all x1, blocking collectives, per_device(): lax.all_to_all(partial, 'pencil', split_axis=0, concat_axis=0, tiled=True)  53.9 us
    pallas_call x1, Pallas kernels, backward(): pl.pallas_call(functools.partial(backward_kernel, height), grid=(width //...  40.4 us
    all_gather x1, blocking collectives, per_device(): row_tiles = lax.all_gather(pair_tile, 'point')  39.7 us
    pallas_call x1, Pallas kernels, forward(): pl.pallas_call(functools.partial(forward_kernel, height), grid=(steps,),...  31.9 us
    all_gather x1, waiting for transfers between devices, per_device(): gathered = lax.all_gather(mixed, 'pencil')  31.1 us
    pallas_call x1, Pallas kernels, mix(): pl.pallas_call(mix_kernel, grid=(own,), out_shape=jax.ShapeDtypeStruct((r...  15.3 us
    pallas_call x1, Pallas kernels, make_terms(): pl.pallas_call(functools.partial(terms_kernel, tiles_dev), out_shape=jax....  11.4 us
    all_to_all x1, starting transfers between devices, per_device(): lax.all_to_all(terms, 'point', split_axis=0, concat_axis=0, tiled=True)  6.32 us
  transfers between devices with their start and end apart: 2, of which 2 were waited for; matrix products, arithmetic and copies ran while one was open for 4% of the time, Pallas kernels for 0%

profile of v1, /device:TPU:0, one launch (start us, length us, event | category | flops | bytes accessed | tf_op | source)
XLA Modules:
  0.0 260.0 jit_solution(4002855909812807152)
XLA Ops:
  6.5 0.0 copy-start.3
  6.5 11.4 %shard_map.73 = bf16[128,64,128]{2,1,0:T(8,128)(2,1)} custom-call(s32[1,64]{1,0:T(1,128)} %counts.1, s32[128]{0:T(128)} %tiles.1, f32[3,128]{1,0:T(4,128)} %offsets.1, bf16[64,8192]{1,0:T(8,128)(2,1)} %features.1, f32[3,8192]{1,0:T(4,128)} %position.1), custom_call_target="tpu_custom_call" | custom-call | tf_op jit(solution)/shard_map/pallas_call | solution.py:75
  17.9 6.3 %all-to-all-start = ((bf16[128,64,128]{2,1,0:T(8,128)(2,1)}), bf16[128,64,128]{2,1,0:T(8,128)(2,1)S(1)}, u32[]{:S(2)}, u32[]{:S(2)}) async-start(bf16[128,64,128]{2,1,0:T(8,128)(2,1)} %shard_map.73), calls=%async_computation | async-start | bytes 4194304 | tf_op jit(solution)/shard_map/all_to_all | solution.py:304
  24.2 0.0 all-gather.5.cloned.1.call-start
  24.2 0.0 copy-done.3
  24.2 39.7 %all-gather.2 = s32[4,1,128]{2,1,0:T(1,128)S(1)} all-gather(s32[1,1,128]{2,1,0:T(1,128)S(1)} %bitcast.24), channel_id=2, replica_groups=mesh['groups'=2,'pencil'=4,'point'=4] {'point'}, dimensions={0}, use_global_device_ids=true | all-gather | bytes 2560 | tf_op jit(solution)/shard_map/all_gather | solution.py:292
  64.0 0.3 reduce_window_sum.11
  64.3 0.1 select_reduce_fusion
  64.5 0.1 sub.34
  64.6 0.1 fusion.21
  64.7 0.1 sine_convert_fusion
  64.9 0.1 copy.16
  65.0 0.2 cosine_convert_fusion.2
  65.2 0.6 pad_maximum_fusion.2
  65.8 0.1 broadcast_compare_fusion
  66.0 0.1 broadcast_in_dim.77
  66.0 0.9 broadcast_select_fusion.y_wave
  66.9 5.6 %all-to-all-done.arrived = bf16[128,64,128]{2,1,0:T(8,128)(2,1)S(1)} async-done(((bf16[128,64,128]{2,1,0:T(8,128)(2,1)}), bf16[128,64,128]{2,1,0:T(8,128)(2,1)S(1)}, u32[]{:S(2)}, u32[]{:S(2)}) %all-to-all-start) | async-done | bytes 2097184 | tf_op jit(solution)/shard_map/all_to_all | solution.py:304
  72.5 0.0 copy-start
  72.5 1.3 copy-done
  73.8 31.9 %shard_map.74 = bf16[64,256,128]{2,1,0:T(8,128)(2,1)} custom-call(bf16[128,64,128]{2,1,0:T(8,128)(2,1)} %copy-done, bf16[1,128,64]{2,1,0:T(8,128)(2,1)} %bitcast.21, bf16[2,512,256]{2,1,0:T(8,128)(2,1)} %broadcast_select_fusion.y_wave), custom_call_target="tpu_custom_call" | custom-call | tf_op jit(solution)/shard_map/pallas_call | solution.py:137
  105.7 53.9 %all_to_all.10 = bf16[64,256,128]{2,1,0:T(8,128)(2,1)} all-to-all(bf16[64,256,128]{2,1,0:T(8,128)(2,1)} %shard_map.74), channel_id=1, replica_groups=mesh['groups'=2,'pencil'=4,'point'=4] {'pencil'}, dimensions={0} | all-to-all | bytes 8388608 | tf_op jit(solution)/shard_map/all_to_all | solution.py:371
  159.6 0.0 copy-start.2
  159.6 0.0 copy-start.1
  159.6 15.3 %shard_map.75 = bf16[256,16,128]{2,1,0:T(8,128)(2,1)} custom-call(bf16[4,16,256,128]{3,2,1,0:T(8,128)(2,1)} %bitcast.16, bf16[16,32,64,128]{3,2,1,0:T(8,128)(2,1)} %weight.1), custom_call_target="tpu_custom_call" | custom-call | tf_op jit(solution)/shard_map/pallas_call | solution.py:181
  174.9 0.0 all-gather.5.cloned.1.call-update
  174.9 0.0 copy-done.2
  174.9 0.1 broadcast_multiply_fusion
  175.1 0.7 mul.222.skip
  175.8 0.1 copy.18
  175.9 0.2 negate_convert_fusion
  176.1 0.7 maximum_maximum_fusion.x_back
  176.9 0.5 multiply_convert_fusion.1
  177.4 0.8 pad_maximum_fusion.y_back
  178.2 0.7 compare_convert_fusion.layer_mask
  178.9 0.0 copy-done.1
  178.9 2.7 %copy.20 = bf16[128,64,128]{2,0,1:T(8,128)(2,1)} copy(bf16[128,64,128]{2,1,0:T(8,128)(2,1)S(1)} %copy-done.1) | data formatting | bytes 4194304 | tf_op jit(solution)/shard_map/all_to_all | solution.py:304
  181.6 31.1 %all-gather.5.cloned.1.call-done = bf16[1024,16,128]{2,1,0:T(8,128)(2,1)} async-done(((bf16[256,16,128]{2,1,0:T(8,128)(2,1)}), bf16[1024,16,128]{2,1,0:T(8,128)(2,1)}) %all-gather.5.cloned.1.call-update) | async-done | bytes 4194320 | tf_op jit(solution)/shard_map/all_gather | solution.py:373
  212.7 40.4 %shard_map.76 = bf16[64,256,512]{2,1,0:T(8,128)(2,1)} custom-call(bf16[4,256,16,128]{3,2,1,0:T(8,128)(2,1)} %bitcast.18, bf16[64,128,128]{2,1,0:T(8,128)(2,1)} %bitcast.17, bf16[128,128]{1,0:T(8,128)(2,1)} %maximum_maximum_fusion.x_back, bf16[256,320]{1,0:T(8,128)(2,1)} %pad_maximum_fusion.y_back, bf16[128,512]{1,0:T(8,128)(2,1)} %compare_convert_fusion.layer_mask, ...), custom_call_target="tpu_custom_call" | custom-call | tf_op jit(solution)/shard_map/pallas_call | solution.py:248
  (15 shorter events, 0.2 us)
Async XLA Ops:
  6.5 17.7 %copy-start.3 = (s32[128]{0:T(128)S(1)}, s32[128]{0:T(128)}, u32[]{:S(2)}) copy-start(s32[128]{0:T(128)} %tiles.1) | copy-start | bytes 1540
  17.9 54.5 %all-to-all-start = ((bf16[128,64,128]{2,1,0:T(8,128)(2,1)}), bf16[128,64,128]{2,1,0:T(8,128)(2,1)S(1)}, u32[]{:S(2)}, u32[]{:S(2)}) async-start(bf16[128,64,128]{2,1,0:T(8,128)(2,1)} %shard_map.73), calls=%async_computation | async-start | bytes 4194304 | tf_op jit(solution)/shard_map/all_to_all | solution.py:304
  24.2 188.5 %all-gather.5.cloned.1.call-start = ((), (), s32[]{:S(2)}) async-start(), calls=%async_computation.2 | async-start | bytes 5242880 | tf_op jit(solution)/shard_map/all_gather | solution.py:373
  72.5 1.3 copy-start
  159.6 15.4 %copy-start.2 = (bf16[64,64]{1,0:T(8,128)(2,1)S(1)}, bf16[64,64]{1,0:T(8,128)(2,1)}, u32[]{:S(2)}) copy-start(bf16[64,64]{1,0:T(8,128)(2,1)} %param.12) | copy-start | bytes 24580
  159.6 19.4 %copy-start.1 = (bf16[128,64,128]{2,1,0:T(8,128)(2,1)S(1)}, bf16[128,64,128]{2,1,0:T(8,128)(2,1)}, u32[]{:S(2)}) copy-start(bf16[128,64,128]{2,1,0:T(8,128)(2,1)} %copy-done) | copy-start | bytes 6291460
Sparse Core Ops, SparseCore 0:
  175.0 37.6 all-gather.4

commit v2 on v1

--- a/solution.py
+++ b/solution.py
@@ -84,73 +84,95 @@
 
 def forward_kernel(height, arrived, x_wave, y_wave, out, held):
     slots, width, lanes = arrived.shape
-    parts, _ = x_wave.shape[1:]
+    parts = x_wave.shape[1]
     steps = parts // 2
     rows = out.shape[1]
+    groups = lanes // LANES
     channels = lanes // height
-    groups = lanes // LANES
+    per_group = LANES // channels
+    stride = held.shape[1] // parts
+    first_half = lax.broadcasted_iota(jnp.int32, (1, LANES), 1) < channels
 
     def one(slot, carry):
-        wave = dot(x_wave[0], arrived[slot])
+        cells = arrived[slot]
+        wave = dot(x_wave[0], jnp.concatenate([cells, cells], axis=0))
         for group in range(groups):
-            held[group, pl.ds(slot, parts, stride=slots), :] = wave[
+            held[group, pl.ds(slot, parts, stride=stride), :] = wave[
                 :, group * LANES : (group + 1) * LANES
             ]
         return carry
 
-    lax.fori_loop(0, slots, one, 0, unroll=4)
-
-    def mode(index, carry):
-        both = [
-            jnp.concatenate(
-                [
-                    held[
-                        group,
-                        pl.ds(pl.multiple_of((index + part * steps) * slots, slots), slots),
-                        :,
-                    ]
-                    for part in range(2)
-                ],
-                axis=0,
+    lax.fori_loop(0, slots, one, 0, unroll=8)
+
+    def both(index, group):
+        return jnp.concatenate(
+            [
+                held[
+                    group,
+                    pl.ds(pl.multiple_of((index + part * steps) * stride, 8), slots),
+                    :,
+                ]
+                for part in range(2)
+            ],
+            axis=0,
+        )
+
+    def modes(index, carry):
+        base = index * 4
+        columns = []
+        for pair in range(2):
+            pieces = []
+            for group in range(groups):
+                left, right = both(base + 2 * pair, group), both(base + 2 * pair + 1, group)
+                left_turned = pltpu.roll(left, channels, 1)
+                right_turned = pltpu.roll(right, channels, 1)
+                pieces.append(jnp.where(first_half, left, right_turned).astype(jnp.bfloat16))
+                pieces.append(jnp.where(first_half, left_turned, right).astype(jnp.bfloat16))
+            columns.append(jnp.concatenate(pieces, axis=0))
+        total = dot(y_wave[...], jnp.concatenate(columns, axis=1))
+        for pair in range(2):
+            real = total[:rows, pair * LANES : (pair + 1) * LANES]
+            imag = total[rows:, pair * LANES : (pair + 1) * LANES]
+            out[base + 2 * pair] = jnp.where(
+                first_half, real, pltpu.roll(imag, channels, 1)
             ).astype(jnp.bfloat16)
-            for group in range(groups)
-        ]
-        real_sum = None
-        for row in range(height):
-            group, first = divmod(row * channels, LANES)
-            piece = dot(y_wave[row], both[group][:, first : first + channels])
-            real_sum = piece if real_sum is None else real_sum + piece
-        out[index] = jnp.concatenate([real_sum[:rows], real_sum[rows:]], axis=1).astype(
-            jnp.bfloat16
-        )
+            out[base + 2 * pair + 1] = jnp.where(
+                first_half, pltpu.roll(real, channels, 1), imag
+            ).astype(jnp.bfloat16)
         return carry
 
-    lax.fori_loop(0, steps, mode, 0, unroll=2)
-
-
-def forward(arrived, x_wave, y_wave, height, chunk):
+    lax.fori_loop(0, steps // 4, modes, 0)
+
+
+def forward(arrived, x_wave, y_wave, height):
     slots, width, lanes = arrived.shape
     channels = lanes // height
-    rows = y_wave.shape[1] // 2
-    steps = KMODES // chunk
+    rows = y_wave.shape[0] // 2
+    steps, double, depth = x_wave.shape
+    chunk = double // 2
     whole = lambda shape: pl.BlockSpec(shape, lambda step: (0,) * len(shape))
+    flops = 2 * steps * double * slots * lanes * (depth + rows)
     return pl.pallas_call(
         functools.partial(forward_kernel, height),
         grid=(steps,),
-        out_shape=jax.ShapeDtypeStruct((KMODES, rows, 2 * channels), jnp.bfloat16),
+        out_shape=jax.ShapeDtypeStruct((steps * chunk, rows, 2 * channels), jnp.bfloat16),
         in_specs=[
             whole(arrived.shape),
-            pl.BlockSpec((1, 2 * chunk, width), lambda step: (step, 0, 0)),
+            pl.BlockSpec((1, double, depth), lambda step: (step, 0, 0)),
             whole(y_wave.shape),
         ],
         out_specs=pl.BlockSpec((chunk, rows, 2 * channels), lambda step: (step, 0, 0)),
-        scratch_shapes=[pltpu.VMEM((lanes // LANES, 2 * chunk * slots, LANES), jnp.float32)],
+        scratch_shapes=[pltpu.VMEM((lanes // LANES, double * (slots + 8), LANES), jnp.float32)],
         compiler_params=pltpu.CompilerParams(vmem_limit_bytes=VMEM_LIMIT),
+        cost_estimate=pl.CostEstimate(
+            flops=flops, bytes_accessed=16 * 1024 * 1024, transcendentals=0
+        ),
     )(arrived, x_wave, y_wave)
 
 
-def mix_kernel(spectra, weight, out, held):
-    sources, _, rows, lanes = spectra.shape
+def mix_kernel(*refs):
+    spectra, (weight, out, held) = refs[:-3], refs[-3:]
+    _, rows, lanes = spectra[0].shape
     count = pl.num_programs(0)
     step = pl.program_id(0)
     stride = held.shape[0] // rows
@@ -160,12 +182,15 @@
     keep = (row < HALF_Z) == (lane < channels)
     for mode in range(MODES):
         at = slice(mode * ZL, (mode + 1) * ZL)
-        total = spectra[0, 0, at].astype(jnp.float32)
-        for source in range(1, sources):
-            total = total + spectra[source, 0, at].astype(jnp.float32)
+        total = spectra[0][0, at].astype(jnp.float32)
+        for source in spectra[1:]:
+            total = total + source[0, at].astype(jnp.float32)
+        high = total.astype(jnp.bfloat16).astype(jnp.float32)
+        split = jnp.concatenate([high, total - high], axis=0).astype(jnp.bfloat16)
         plain = weight[0, mode]
         turned = jnp.concatenate([-plain[:, channels:], plain[:, :channels]], axis=1)
-        mixed = dot(total.astype(jnp.bfloat16), jnp.concatenate([plain, turned], axis=0))
+        mixed = dot(split, jnp.concatenate([plain, turned], axis=0))
+        mixed = mixed[:ZL] + mixed[ZL:]
         other = pltpu.roll(pltpu.roll(mixed, HALF_Z, 0), channels, 1)
         held[pl.ds(mode * ZL * stride + step, ZL, stride=stride), :] = jnp.where(
             keep, mixed, other
@@ -177,19 +202,19 @@
 
 
 def mix(spectra, weight):
-    sources, own, rows, lanes = spectra.shape
+    own, rows, lanes = spectra[0].shape
     return pl.pallas_call(
         mix_kernel,
         grid=(own,),
         out_shape=jax.ShapeDtypeStruct((rows, own, lanes), jnp.bfloat16),
         in_specs=[
-            pl.BlockSpec((sources, 1, rows, lanes), lambda step: (0, step, 0, 0)),
+            *[pl.BlockSpec((1, rows, lanes), lambda step: (step, 0, 0)) for _ in spectra],
             pl.BlockSpec((1,) + weight.shape[1:], lambda step: (step, 0, 0, 0)),
         ],
         out_specs=pl.BlockSpec((rows, own, lanes), lambda step: (0, 0, 0)),
         scratch_shapes=[pltpu.VMEM((rows * own, lanes), jnp.float32)],
         compiler_params=pltpu.CompilerParams(vmem_limit_bytes=VMEM_LIMIT),
-    )(spectra, weight)
+    )(*spectra, weight)
 
 
 def backward_kernel(height, mixed, terms, x_back, y_back, layer_mask, skip, out, held):
@@ -211,14 +236,16 @@
                     ],
                     axis=0,
                 )
-                held[layer, pl.ds(index, 2 * width, stride=MODES), :] = dot(x_back[...], modes)
+                held[layer, pl.ds(index, 2 * width, stride=MODES), :] = dot(
+                    x_back[...], jnp.concatenate([modes, modes], axis=0)
+                )
             return carry
 
         lax.fori_loop(0, MODES, mode, 0, unroll=2)
 
     for inner in range(per_step):
         x = step * per_step + inner
-        parts = [
+        wave = [
             jnp.concatenate(
                 [
                     held[
@@ -229,9 +256,12 @@
                     for layer in range(HALF_Z)
                 ],
                 axis=1,
-            ).astype(jnp.bfloat16)
+            )
             for part in range(2)
         ]
+        wave = jnp.concatenate(wave, axis=0)
+        high = wave.astype(jnp.bfloat16)
+        parts = [high, (wave - high.astype(jnp.float32)).astype(jnp.bfloat16), high]
         skipped = dot(terms[inner], skip[...]).astype(jnp.bfloat16)
         for row in range(height):
             piece = skipped[:, row * channels : (row + 1) * channels]
@@ -261,6 +291,12 @@
         scratch_shapes=[pltpu.VMEM((HALF_Z, 2 * width * MODES, mixed.shape[3]), jnp.float32)],
         compiler_params=pltpu.CompilerParams(vmem_limit_bytes=VMEM_LIMIT),
     )(mixed, terms, x_back, y_back, layer_mask, skip)
+
+
+def split(value, axis):
+    high = value.astype(jnp.bfloat16)
+    low = (value - high.astype(jnp.float32)).astype(jnp.bfloat16)
+    return jnp.concatenate([high, low], axis=axis)
 
 
 def angle(phase, length):
@@ -287,6 +323,7 @@
     tiles_dev = ZL * row_blocks
     slots = owners * CAP
     own = KMODES // pencils
+    lanes = height * channels
     bf16 = jnp.bfloat16
 
     row_tiles = lax.all_gather(pair_tile, "point")
@@ -318,22 +355,27 @@
     x_cells = pencil * width + jnp.arange(width, dtype=jnp.int32)
     x_angle = angle(x_freqs[:, None] * x_cells[None, :], NX)
     x_cos, x_sin = jnp.cos(x_angle), jnp.sin(x_angle)
-    chunk = KMODES if slots * height * channels * KMODES * 8 <= 16 * 1024 * 1024 else 8
-    steps = KMODES // chunk
-    x_wave = (
-        jnp.stack([x_cos, -x_sin])
-        .reshape(2, steps, chunk, width)
-        .transpose(1, 0, 2, 3)
-        .reshape(steps, 2 * chunk, width)
-        .astype(bf16)
-    )
+    cores = 2
+    chips = pencils // cores
+    chip, core = pencil // cores, pencil % cores
+    chunk = own if slots * lanes * own * 8 <= 8 * 1024 * 1024 else 4
+
+    def x_wave(dests):
+        index = jnp.concatenate([dest * own + jnp.arange(own, dtype=jnp.int32) for dest in dests])
+        phase = angle(x_freqs[index][:, None] * x_cells[None, :], NX)
+        steps = index.shape[0] // chunk
+        table = split(jnp.stack([jnp.cos(phase), -jnp.sin(phase)]), 2)
+        table = table.reshape(2, steps, chunk, 2 * width).transpose(1, 0, 2, 3)
+        return table.reshape(steps, 2 * chunk, 2 * width)
+
     x_back = jnp.concatenate(
         [
             jnp.concatenate([x_cos.T, -x_sin.T], axis=1),
             jnp.concatenate([x_sin.T, x_cos.T], axis=1),
         ],
         axis=0,
-    ).astype(bf16)
+    )
+    x_back = split(x_back, 1)
 
     pair_y = block_of[None, :] * height + jnp.arange(height, dtype=jnp.int32)[:, None]
     y_angle = angle(modes[None, :, None] * pair_y[:, None, :], NY)
@@ -350,15 +392,20 @@
     )
     y_wave = jnp.where(
         layer_hit[None, None, None, :, None, :], turned[:, :, :, None], jnp.zeros((), bf16)
-    ).reshape(height, 2 * MODES * ZL, 2 * slots)
+    )
+    y_wave = y_wave.transpose(1, 2, 3, 0, 4, 5).reshape(2 * MODES * ZL, height * 2 * slots)
 
     rows_y = jnp.arange(NY, dtype=jnp.int32)
     back_angle = angle(rows_y[:, None] * modes[None, :], NY)
     scale = jnp.where(modes == 0, 1.0, 2.0).astype(jnp.float32)[None, :] / (NX * NY)
+    wave_back = jnp.concatenate([jnp.cos(back_angle), -jnp.sin(back_angle)], axis=1)
+    wave_back = wave_back * jnp.concatenate([scale, scale], axis=1)
+    wave_high = wave_back.astype(bf16)
     y_back = jnp.concatenate(
         [
-            (jnp.cos(back_angle) * scale).astype(bf16),
-            (-jnp.sin(back_angle) * scale).astype(bf16),
+            wave_high,
+            wave_high,
+            (wave_back - wave_high.astype(jnp.float32)).astype(bf16),
             (rows_y[:, None] == pair_y.reshape(-1)[None, :]).astype(bf16),
         ],
         axis=1,
@@ -367,9 +414,27 @@
     layer_mask = (layer_of[:, None] == lane_layer[None, :]).astype(bf16)
     skip = jnp.kron(jnp.eye(height, dtype=bf16), skip_weight)
 
-    partial = forward(arrived, x_wave, y_wave, height, chunk)
-    spectra = lax.all_to_all(partial, "pencil", split_axis=0, concat_axis=0, tiled=True)
-    mixed = mix(spectra.reshape(pencils, own, MODES * ZL, 2 * channels), spectral_weight)
+    def to_core(value):
+        return lax.ppermute(
+            value, "pencil", [(rank, rank // cores * cores + 1 - rank % cores) for rank in range(pencils)]
+        )
+
+    def dest(shift, other):
+        return (chip + shift) % chips * cores + (1 - core if other else core)
+
+    shifts = list(range(1, chips))
+    for_other = forward(arrived, x_wave([dest(shift, True) for shift in shifts]), y_wave, height)
+    from_other = to_core(for_other)
+    for_own = forward(arrived, x_wave([dest(shift, False) for shift in shifts]), y_wave, height)
+    sums = (for_own.astype(jnp.float32) + from_other.astype(jnp.float32)).astype(bf16)
+    near = forward(arrived, x_wave([dest(0, True), dest(0, False)]), y_wave, height)
+    spectra = [near[own:], to_core(near[:own])]
+    for place, shift in enumerate(shifts):
+        moves = [
+            (rank, (rank // cores + shift) % chips * cores + rank % cores) for rank in range(pencils)
+        ]
+        spectra.append(lax.ppermute(sums[place * own : (place + 1) * own], "pencil", moves))
+    mixed = mix(spectra, spectral_weight)
     gathered = lax.all_gather(mixed, "pencil")
     by_row = arrived.transpose(1, 0, 2)
     return backward(

time: 261 us -> 238 us (0.912)
  blocking collectives: 93.6 us -> 39.7 us
  waiting for transfers between devices: 36.7 us -> 60.9 us
  local copies, waits for them, and re-layouts: 5.09 us -> 10.8 us
  Pallas kernels: 99 us -> 94.2 us
  other arithmetic: 5.74 us -> 9.24 us
    all_to_all x1 -> x0, blocking collectives: 53.9 us -> none  [per_device(): lax.all_to_all(partial, 'pencil', split_axis=0, concat_axis=0, tiled=True)]
    ppermute x0 -> x3, waiting for transfers between devices: none -> 23.6 us  [the longest x1 23.6 us: per_device(): lax.ppermute(sums[place * own:(place + 1) * own], 'pencil', moves)]
    pallas_call x1 -> x3, Pallas kernels: 31.9 us -> 27.6 us  [forward(): pl.pallas_call(functools.partial(forward_kernel, height), grid=(steps,),...]
    all_gather x1, waiting for transfers between devices: 31.1 us -> 33.9 us  [per_device(): gathered = lax.all_gather(mixed, 'pencil')]
    slice x0 -> x1, local copies, waits for them, and re-layouts: none -> 2.74 us  [per_device(): spectra = [near[own:], to_core(near[:own])]]
  transfers between devices with their start and end apart: 2 -> 5, of which waited for: 2 -> 3; matrix products, arithmetic and copies ran while one was open for 4% -> 7% of each run, Pallas kernels for 0% -> 8%
where the time goes in v2:
time: 238 us; the launch traced here: 237 us
  Pallas kernels  94.2 us (40%)
  waiting for transfers between devices  60.9 us (26%)
  blocking collectives  39.7 us (17%)
  between operations  13.6 us (6%)
  local copies, waits for them, and re-layouts  10.8 us (5%)
  other arithmetic  9.24 us (4%)
  starting transfers between devices  8.48 us (4%)
    pallas_call x1, Pallas kernels, backward(): pl.pallas_call(functools.partial(backward_kernel, height), grid=(width //...  40.2 us
    all_gather x1, blocking collectives, per_device(): row_tiles = lax.all_gather(pair_tile, 'point')  39.7 us
    all_gather x1, waiting for transfers between devices, per_device(): gathered = lax.all_gather(mixed, 'pencil')  33.9 us
    pallas_call x3, Pallas kernels, forward(): pl.pallas_call(functools.partial(forward_kernel, height), grid=(steps,),...  27.6 us
    ppermute x1, waiting for transfers between devices, per_device(): lax.ppermute(sums[place * own:(place + 1) * own], 'pencil', moves)  23.6 us
    pallas_call x1, Pallas kernels, mix(): pl.pallas_call(mix_kernel, grid=(own,), out_shape=jax.ShapeDtypeStruct((r...  15.1 us
    pallas_call x1, Pallas kernels, make_terms(): pl.pallas_call(functools.partial(terms_kernel, tiles_dev), out_shape=jax....  11.4 us
    all_to_all x1, starting transfers between devices, per_device(): lax.all_to_all(terms, 'point', split_axis=0, concat_axis=0, tiled=True)  6.45 us
  transfers between devices with their start and end apart: 5, of which 3 were waited for; matrix products, arithmetic and copies ran while one was open for 7% of the time, Pallas kernels for 8%

profile of v2, /device:TPU:0, one launch (start us, length us, event | category | flops | bytes accessed | tf_op | source)
XLA Modules:
  0.0 237.0 jit_solution(3838536503961563779)
XLA Ops:
  6.5 11.4 %shard_map.73 = bf16[128,64,128]{2,1,0:T(8,128)(2,1)} custom-call(s32[1,64]{1,0:T(1,128)} %counts.1, s32[128]{0:T(128)} %tiles.1, f32[3,128]{1,0:T(4,128)} %offsets.1, bf16[64,8192]{1,0:T(8,128)(2,1)} %features.1, f32[3,8192]{1,0:T(4,128)} %position.1), custom_call_target="tpu_custom_call" | custom-call | tf_op jit(solution)/shard_map/pallas_call | solution.py:75
  17.9 0.0 copy-start.5
  17.9 6.4 %all-to-all-start = ((bf16[128,64,128]{2,1,0:T(8,128)(2,1)}), bf16[128,64,128]{2,1,0:T(8,128)(2,1)S(1)}, u32[]{:S(2)}, u32[]{:S(2)}) async-start(bf16[128,64,128]{2,1,0:T(8,128)(2,1)} %shard_map.73), calls=%async_computation | async-start | bytes 4194304 | tf_op jit(solution)/shard_map/all_to_all | solution.py:341
  24.3 0.0 all-gather.5.cloned.1.call-start
  24.4 0.0 copy-done.5
  24.4 39.7 %all-gather.2 = s32[4,1,128]{2,1,0:T(1,128)S(1)} all-gather(s32[1,1,128]{2,1,0:T(1,128)S(1)} %bitcast.54), channel_id=2, replica_groups=mesh['groups'=2,'pencil'=4,'point'=4] {'point'}, dimensions={0}, use_global_device_ids=true | all-gather | bytes 2560 | tf_op jit(solution)/shard_map/all_gather | solution.py:329
  64.1 0.3 reduce_window_sum.11
  64.4 0.1 select_reduce_fusion
  64.6 0.1 sub.75
  64.7 0.1 fusion.48
  64.8 0.7 gather_fusion
  65.5 0.1 mul.298
  65.6 0.7 gather_fusion.2
  66.3 0.7 gather_fusion.1
  66.9 0.1 fusion.36
  67.1 0.1 sine_convert_fusion
  67.3 0.1 copy.20
  67.4 0.2 fusion.35
  67.6 0.7 pad_maximum_fusion.7.x_wave
  68.2 0.1 broadcast_compare_fusion
  68.3 0.9 broadcast_select_fusion
  69.2 3.4 %all-to-all-done.arrived = bf16[128,64,128]{2,1,0:T(8,128)(2,1)S(1)} async-done(((bf16[128,64,128]{2,1,0:T(8,128)(2,1)}), bf16[128,64,128]{2,1,0:T(8,128)(2,1)S(1)}, u32[]{:S(2)}, u32[]{:S(2)}) %all-to-all-start) | async-done | bytes 2097184 | tf_op jit(solution)/shard_map/all_to_all | solution.py:341
  72.6 0.0 copy-start
  72.6 1.3 copy-done
  73.9 7.6 %shard_map.76 = bf16[16,256,128]{2,1,0:T(8,128)(2,1)} custom-call(bf16[128,64,128]{2,1,0:T(8,128)(2,1)} %copy-done, bf16[1,32,128]{2,1,0:T(8,128)(2,1)} %pad_maximum_fusion.7.x_wave, bf16[512,512]{1,0:T(8,128)(2,1)} %bitcast.44), custom_call_target="tpu_custom_call" | custom-call | flops 402653184 | bytes 16777216 | tf_op jit(solution)/shard_map/pallas_call | solution.py:155
  81.5 0.0 collective-permute-start.1
  81.5 0.7 pad_maximum_fusion.6.x_wave
  82.1 0.2 fusion.33
  82.3 0.7 pad_maximum_fusion.3
  83.0 12.5 %shard_map.74 = bf16[32,256,128]{2,1,0:T(8,128)(2,1)} custom-call(bf16[128,64,128]{2,1,0:T(8,128)(2,1)} %copy-done, bf16[2,32,128]{2,1,0:T(8,128)(2,1)} %bitcast.49, bf16[512,512]{1,0:T(8,128)(2,1)} %bitcast.45), custom_call_target="tpu_custom_call" | custom-call | flops 805306368 | bytes 16777216 | tf_op jit(solution)/shard_map/pallas_call | solution.py:155
  95.5 2.7 %fusion.53 = (bf16[16,256,128]{2,1,0:T(8,128)(2,1)S(1)}, bf16[16,256,128]{2,1,0:T(8,128)(2,1)}) fusion(bf16[32,256,128]{2,1,0:T(8,128)(2,1)} %shard_map.74), kind=kLoop, calls=%fused_computation.156 | loop fusion | bytes 4194304 | tf_op jit(solution)/shard_map/slice | solution.py:431
  98.2 0.5 collective-permute-start
  98.7 7.6 %shard_map.75 = bf16[16,256,128]{2,1,0:T(8,128)(2,1)} custom-call(bf16[128,64,128]{2,1,0:T(8,128)(2,1)} %copy-done, bf16[1,32,128]{2,1,0:T(8,128)(2,1)} %pad_maximum_fusion.6.x_wave, bf16[512,512]{1,0:T(8,128)(2,1)} %bitcast.46), custom_call_target="tpu_custom_call" | custom-call | flops 402653184 | bytes 16777216 | tf_op jit(solution)/shard_map/pallas_call | solution.py:155
  106.3 0.0 collective-permute-done.1
  106.3 1.5 add_convert_fusion
  107.8 1.6 collective-permute-start.2
  109.4 0.0 collective-permute-done.refs_1_
  109.4 0.0 copy-start.2
  109.4 23.6 %collective-permute-done.2.refs_2_ = bf16[16,256,128]{2,1,0:T(8,128)(2,1)S(1)} collective-permute-done((bf16[16,256,128]{2,1,0:T(8,128)(2,1)S(1)}, bf16[16,256,128]{2,1,0:T(8,128)(2,1)S(1)}, u32[]{:S(2)}, u32[]{:S(2)}) %collective-permute-start.2) | collective-permute-done | bytes 1048608 | tf_op jit(solution)/shard_map/ppermute | solution.py:436
  133.0 0.0 copy-start.3
  133.0 0.0 copy-done.2
  133.0 1.0 copy-done.3
  134.0 0.0 copy-start.4
  134.0 15.1 %shard_map.77 = bf16[256,16,128]{2,1,0:T(8,128)(2,1)} custom-call(bf16[16,256,128]{2,1,0:T(8,128)(2,1)} %get-tuple-element.12.refs_0_, bf16[16,256,128]{2,1,0:T(8,128)(2,1)} %copy-done.2, bf16[16,256,128]{2,1,0:T(8,128)(2,1)} %copy-done.3, bf16[16,32,64,128]{3,2,1,0:T(8,128)(2,1)} %refs_3_.1), custom_call_target="tpu_custom_call" | custom-call | tf_op jit(solution)/shard_map/pallas_call | solution.py:206
  149.1 0.0 copy-start.1
  149.1 0.0 all-gather.5.cloned.1.call-update
  149.1 0.0 copy-done.4
  149.1 0.1 broadcast_multiply_fusion
  149.2 0.7 mul.339.skip
  150.0 0.1 copy.22
  150.1 0.1 maximum_bitcast_fusion.3
  150.2 0.2 fusion.26
  150.4 0.1 subtract_convert_fusion.1
  150.5 0.1 fusion.18
  150.6 0.6 pad_maximum_fusion.1.x_back
  151.2 0.5 multiply_cosine_fusion
  151.7 0.1 fusion.2
  151.8 0.9 pad_maximum_fusion.y_back
  152.7 0.7 compare_convert_fusion.layer_mask
  153.4 0.0 copy-done.1
  153.4 2.7 %copy.24 = bf16[128,64,128]{2,0,1:T(8,128)(2,1)} copy(bf16[128,64,128]{2,1,0:T(8,128)(2,1)S(1)} %copy-done.1) | data formatting | bytes 4194304 | tf_op jit(solution)/shard_map/all_to_all | solution.py:341
  156.1 33.9 %all-gather.5.cloned.1.call-done = bf16[1024,16,128]{2,1,0:T(8,128)(2,1)} async-done(((bf16[256,16,128]{2,1,0:T(8,128)(2,1)}), bf16[1024,16,128]{2,1,0:T(8,128)(2,1)}) %all-gather.5.cloned.1.call-update) | async-done | bytes 4194320 | tf_op jit(solution)/shard_map/all_gather | solution.py:438
  190.0 40.2 %shard_map.78 = bf16[64,256,512]{2,1,0:T(8,128)(2,1)} custom-call(bf16[4,256,16,128]{3,2,1,0:T(8,128)(2,1)} %bitcast.48, bf16[64,128,128]{2,1,0:T(8,128)(2,1)} %bitcast.47, bf16[128,256]{1,0:T(8,128)(2,1)} %pad_maximum_fusion.1.x_back, bf16[256,448]{1,0:T(8,128)(2,1)} %pad_maximum_fusion.y_back, bf16[128,512]{1,0:T(8,128)(2,1)} %compare_convert_fusion.layer_mask, ...), custom_call_target="tpu_custom_call" | custom-call | tf_op jit(solution)/shard_map/pallas_call | solution.py:278
  (26 shorter events, 0.2 us)
Async XLA Ops:
  17.9 6.5 %copy-start.5 = (s32[128]{0:T(128)S(1)}, s32[128]{0:T(128)}, u32[]{:S(2)}) copy-start(s32[128]{0:T(128)} %tiles.1) | copy-start | bytes 1540
  17.9 54.7 %all-to-all-start = ((bf16[128,64,128]{2,1,0:T(8,128)(2,1)}), bf16[128,64,128]{2,1,0:T(8,128)(2,1)S(1)}, u32[]{:S(2)}, u32[]{:S(2)}) async-start(bf16[128,64,128]{2,1,0:T(8,128)(2,1)} %shard_map.73), calls=%async_computation | async-start | bytes 4194304 | tf_op jit(solution)/shard_map/all_to_all | solution.py:341
  24.3 165.6 %all-gather.5.cloned.1.call-start = ((), (), s32[]{:S(2)}) async-start(), calls=%async_computation.1 | async-start | bytes 5242880 | tf_op jit(solution)/shard_map/all_gather | solution.py:438
  72.6 1.3 copy-start
  81.5 24.8 %collective-permute-start.1 = (bf16[16,256,128]{2,1,0:T(8,128)(2,1)}, bf16[16,256,128]{2,1,0:T(8,128)(2,1)S(1)}, u32[]{:S(2)}, u32[]{:S(2)}) collective-permute-start(bf16[16,256,128]{2,1,0:T(8,128)(2,1)} %shard_map.76), channel_id=1, source_target_pairs={{0,4},{4,0},{8,12},{12,8},{1,5},{5,1},{9,13},{13,9},{2,6},{6,2},{1... | collective-permute-start | bytes 3145736 | tf_op jit(solution)/shard_map/ppermute | solution.py:418
  98.2 11.1 %collective-permute-start = (bf16[16,256,128]{2,1,0:T(8,128)(2,1)S(1)}, bf16[16,256,128]{2,1,0:T(8,128)(2,1)S(1)}, u32[]{:S(2)}, u32[]{:S(2)}) collective-permute-start(bf16[16,256,128]{2,1,0:T(8,128)(2,1)S(1)} %get-tuple-element.11), channel_id=1, source_target_pairs={{0,4},{4,0},{8,12},{12,8},{1,5},{5,1},{9,13},{13,9},{2,6},{6,2},{1... | collective-permute-start | bytes 3145736 | tf_op jit(solution)/shard_map/ppermute | solution.py:418
  107.8 25.2 %collective-permute-start.2 = (bf16[16,256,128]{2,1,0:T(8,128)(2,1)S(1)}, bf16[16,256,128]{2,1,0:T(8,128)(2,1)S(1)}, u32[]{:S(2)}, u32[]{:S(2)}) collective-permute-start(bf16[16,256,128]{2,1,0:T(8,128)(2,1)S(1)} %add_convert_fusion), channel_id=1, source_target_pairs={{0,8},{4,12},{8,0},{12,4},{1,9},{5,13},{9,1},{13,5},{2,10},{6,14},... | collective-permute-start | bytes 3145736 | tf_op jit(solution)/shard_map/ppermute | solution.py:436
  109.4 23.6 %copy-start.2 = (bf16[16,256,128]{2,1,0:T(8,128)(2,1)}, bf16[16,256,128]{2,1,0:T(8,128)(2,1)S(1)}, u32[]{:S(2)}) copy-start(bf16[16,256,128]{2,1,0:T(8,128)(2,1)S(1)} %collective-permute-done.refs_1_) | copy-start | bytes 3145732
  133.0 1.0 copy-start.3
  134.0 15.1 %copy-start.4 = (bf16[64,64]{1,0:T(8,128)(2,1)S(1)}, bf16[64,64]{1,0:T(8,128)(2,1)}, u32[]{:S(2)}) copy-start(bf16[64,64]{1,0:T(8,128)(2,1)} %param.12) | copy-start | bytes 24580
  149.1 4.4 %copy-start.1 = (bf16[128,64,128]{2,1,0:T(8,128)(2,1)S(1)}, bf16[128,64,128]{2,1,0:T(8,128)(2,1)}, u32[]{:S(2)}) copy-start(bf16[128,64,128]{2,1,0:T(8,128)(2,1)} %copy-done) | copy-start | bytes 6291460
Sparse Core Ops, SparseCore 0:
  149.2 40.7 all-gather.4

commit v3 on v2

--- a/solution.py
+++ b/solution.py
@@ -427,7 +427,8 @@
     from_other = to_core(for_other)
     for_own = forward(arrived, x_wave([dest(shift, False) for shift in shifts]), y_wave, height)
     sums = (for_own.astype(jnp.float32) + from_other.astype(jnp.float32)).astype(bf16)
-    near = forward(arrived, x_wave([dest(0, True), dest(0, False)]), y_wave, height)
+    later, sums = lax.optimization_barrier((arrived, sums))
+    near = forward(later, x_wave([dest(0, True), dest(0, False)]), y_wave, height)
     spectra = [near[own:], to_core(near[:own])]
     for place, shift in enumerate(shifts):
         moves = [

time: 238 us -> 223 us (0.937)
  waiting for transfers between devices: 60.9 us -> 46 us
    ppermute x1, waiting for transfers between devices: 23.6 us -> 8.71 us  [per_device(): lax.ppermute(sums[place * own:(place + 1) * own], 'pencil', moves)]
  transfers between devices with their start and end apart: 5 -> 5, of which waited for: 3 -> 3; matrix products, arithmetic and copies ran while one was open for 7% -> 7% of each run, Pallas kernels for 8% -> 9%
where the time goes in v3:
time: 223 us; the launch traced here: 222 us
  Pallas kernels  94.2 us (42%)
  waiting for transfers between devices  46 us (21%)
  blocking collectives  39.7 us (18%)
  between operations  13.6 us (6%)
  local copies, waits for them, and re-layouts  11.1 us (5%)
  other arithmetic  9.25 us (4%)
  starting transfers between devices  8.24 us (4%)
    pallas_call x1, Pallas kernels, backward(): pl.pallas_call(functools.partial(backward_kernel, height), grid=(width //...  40.2 us
    all_gather x1, blocking collectives, per_device(): row_tiles = lax.all_gather(pair_tile, 'point')  39.7 us
    all_gather x1, waiting for transfers between devices, per_device(): gathered = lax.all_gather(mixed, 'pencil')  33.1 us
    pallas_call x3, Pallas kernels, forward(): pl.pallas_call(functools.partial(forward_kernel, height), grid=(steps,),...  27.6 us
    pallas_call x1, Pallas kernels, mix(): pl.pallas_call(mix_kernel, grid=(own,), out_shape=jax.ShapeDtypeStruct((r...  15.1 us
    pallas_call x1, Pallas kernels, make_terms(): pl.pallas_call(functools.partial(terms_kernel, tiles_dev), out_shape=jax....  11.4 us
    ppermute x1, waiting for transfers between devices, per_device(): lax.ppermute(sums[place * own:(place + 1) * own], 'pencil', moves)  8.71 us
    all_to_all x1, starting transfers between devices, per_device(): lax.all_to_all(terms, 'point', split_axis=0, concat_axis=0, tiled=True)  6.45 us
  transfers between devices with their start and end apart: 5, of which 3 were waited for; matrix products, arithmetic and copies ran while one was open for 7% of the time, Pallas kernels for 9%

profile of v3, /device:TPU:0, one launch (start us, length us, event | category | flops | bytes accessed | tf_op | source)
XLA Modules:
  0.0 222.1 jit_solution(18051564977893827596)
XLA Ops:
  6.5 11.4 %shard_map.73 = bf16[128,64,128]{2,1,0:T(8,128)(2,1)} custom-call(s32[1,64]{1,0:T(1,128)} %counts.1, s32[128]{0:T(128)} %tiles.1, f32[3,128]{1,0:T(4,128)} %offsets.1, bf16[64,8192]{1,0:T(8,128)(2,1)} %features.1, f32[3,8192]{1,0:T(4,128)} %position.1), custom_call_target="tpu_custom_call" | custom-call | tf_op jit(solution)/shard_map/pallas_call | solution.py:75
  17.9 0.0 copy-start.5
  17.9 6.4 %all-to-all-start = ((bf16[128,64,128]{2,1,0:T(8,128)(2,1)}), bf16[128,64,128]{2,1,0:T(8,128)(2,1)S(1)}, u32[]{:S(2)}, u32[]{:S(2)}) async-start(bf16[128,64,128]{2,1,0:T(8,128)(2,1)} %shard_map.73), calls=%async_computation | async-start | bytes 4194304 | tf_op jit(solution)/shard_map/all_to_all | solution.py:341
  24.3 0.0 all-gather.5.cloned.1.call-start
  24.4 0.0 copy-done.5
  24.4 39.7 %all-gather.2 = s32[4,1,128]{2,1,0:T(1,128)S(1)} all-gather(s32[1,1,128]{2,1,0:T(1,128)S(1)} %bitcast.54), channel_id=2, replica_groups=mesh['groups'=2,'pencil'=4,'point'=4] {'point'}, dimensions={0}, use_global_device_ids=true | all-gather | bytes 2560 | tf_op jit(solution)/shard_map/all_gather | solution.py:329
  64.1 0.3 reduce_window_sum.11
  64.4 0.1 select_reduce_fusion
  64.6 0.1 sub.74
  64.7 0.7 gather_fusion.1
  65.4 0.7 gather_fusion
  66.1 0.1 fusion.36
  66.2 0.1 sine_convert_fusion
  66.4 0.1 copy.20
  66.5 0.1 fusion.50
  66.6 0.2 fusion.35
  66.8 0.7 pad_maximum_fusion.7.x_wave
  67.4 0.1 broadcast_compare_fusion
  67.5 0.9 broadcast_select_fusion
  68.4 4.2 %all-to-all-done.arrived = bf16[128,64,128]{2,1,0:T(8,128)(2,1)S(1)} async-done(((bf16[128,64,128]{2,1,0:T(8,128)(2,1)}), bf16[128,64,128]{2,1,0:T(8,128)(2,1)S(1)}, u32[]{:S(2)}, u32[]{:S(2)}) %all-to-all-start) | async-done | bytes 2097184 | tf_op jit(solution)/shard_map/all_to_all | solution.py:341
  72.6 0.0 copy-start
  72.6 1.3 copy-done
  73.9 7.6 %shard_map.75 = bf16[16,256,128]{2,1,0:T(8,128)(2,1)} custom-call(bf16[128,64,128]{2,1,0:T(8,128)(2,1)} %copy-done, bf16[1,32,128]{2,1,0:T(8,128)(2,1)} %pad_maximum_fusion.7.x_wave, bf16[512,512]{1,0:T(8,128)(2,1)} %bitcast.44), custom_call_target="tpu_custom_call" | custom-call | flops 402653184 | bytes 16777216 | tf_op jit(solution)/shard_map/pallas_call | solution.py:155
  81.5 0.0 collective-permute-start
  81.5 0.7 gather_fusion.2
  82.2 0.1 mul.317
  82.3 0.7 pad_maximum_fusion.6.x_wave
  82.9 0.2 fusion.33
  83.1 0.7 pad_maximum_fusion.5
  83.8 7.6 %shard_map.74 = bf16[16,256,128]{2,1,0:T(8,128)(2,1)} custom-call(bf16[128,64,128]{2,1,0:T(8,128)(2,1)} %copy-done, bf16[1,32,128]{2,1,0:T(8,128)(2,1)} %pad_maximum_fusion.6.x_wave, bf16[512,512]{1,0:T(8,128)(2,1)} %bitcast.45), custom_call_target="tpu_custom_call" | custom-call | flops 402653184 | bytes 16777216 | tf_op jit(solution)/shard_map/pallas_call | solution.py:155
  91.4 0.0 collective-permute-done
  91.4 1.5 add_convert_fusion
  92.9 1.6 collective-permute-start.2
  94.5 12.4 %shard_map.76 = bf16[32,256,128]{2,1,0:T(8,128)(2,1)} custom-call(bf16[128,64,128]{2,1,0:T(8,128)(2,1)} %copy-done, bf16[2,32,128]{2,1,0:T(8,128)(2,1)} %bitcast.49, bf16[512,512]{1,0:T(8,128)(2,1)} %bitcast.46), custom_call_target="tpu_custom_call" | custom-call | flops 805306368 | bytes 16777216 | tf_op jit(solution)/shard_map/pallas_call | solution.py:155
  106.9 2.7 %fusion.53 = (bf16[16,256,128]{2,1,0:T(8,128)(2,1)S(1)}, bf16[16,256,128]{2,1,0:T(8,128)(2,1)}) fusion(bf16[32,256,128]{2,1,0:T(8,128)(2,1)} %shard_map.76), kind=kLoop, calls=%fused_computation.156 | loop fusion | bytes 4194304 | tf_op jit(solution)/shard_map/slice | solution.py:432
  109.6 0.2 collective-permute-start.1
  109.8 8.7 %collective-permute-done.2.refs_2_ = bf16[16,256,128]{2,1,0:T(8,128)(2,1)S(1)} collective-permute-done((bf16[16,256,128]{2,1,0:T(8,128)(2,1)S(1)}, bf16[16,256,128]{2,1,0:T(8,128)(2,1)S(1)}, u32[]{:S(2)}, u32[]{:S(2)}) %collective-permute-start.2) | collective-permute-done | bytes 1048608 | tf_op jit(solution)/shard_map/ppermute | solution.py:437
  118.5 0.0 copy-start.2
  118.5 0.0 collective-permute-done.1.refs_1_
  118.5 0.0 copy-start.3
  118.5 1.0 copy-done.2
  119.5 0.4 copy-done.3
  119.9 0.0 copy-start.4
  119.9 15.1 %shard_map.77 = bf16[256,16,128]{2,1,0:T(8,128)(2,1)} custom-call(bf16[16,256,128]{2,1,0:T(8,128)(2,1)} %get-tuple-element.16.refs_0_, bf16[16,256,128]{2,1,0:T(8,128)(2,1)} %copy-done.3, bf16[16,256,128]{2,1,0:T(8,128)(2,1)} %copy-done.2, bf16[16,32,64,128]{3,2,1,0:T(8,128)(2,1)} %refs_3_.1), custom_call_target="tpu_custom_call" | custom-call | tf_op jit(solution)/shard_map/pallas_call | solution.py:206
  135.0 0.0 copy-start.1
  135.0 0.0 all-gather.5.cloned.1.call-update
  135.0 0.0 copy-done.4
  135.0 0.1 broadcast_multiply_fusion
  135.1 0.7 mul.339.skip
  135.9 0.1 copy.22
  136.0 0.1 maximum_bitcast_fusion.3
  136.1 0.2 fusion.26
  136.3 0.1 subtract_convert_fusion.1
  136.4 0.1 fusion.18
  136.5 0.6 pad_maximum_fusion.1.x_back
  137.1 0.5 multiply_cosine_fusion
  137.6 0.1 fusion.2
  137.7 0.9 pad_maximum_fusion.y_back
  138.6 0.7 compare_convert_fusion.layer_mask
  139.3 0.0 copy-done.1
  139.3 2.7 %copy.24 = bf16[128,64,128]{2,0,1:T(8,128)(2,1)} copy(bf16[128,64,128]{2,1,0:T(8,128)(2,1)S(1)} %copy-done.1) | data formatting | bytes 4194304 | tf_op jit(solution)/shard_map/all_to_all | solution.py:341
  142.0 33.1 %all-gather.5.cloned.1.call-done = bf16[1024,16,128]{2,1,0:T(8,128)(2,1)} async-done(((bf16[256,16,128]{2,1,0:T(8,128)(2,1)}), bf16[1024,16,128]{2,1,0:T(8,128)(2,1)}) %all-gather.5.cloned.1.call-update) | async-done | bytes 4194320 | tf_op jit(solution)/shard_map/all_gather | solution.py:439
  175.1 40.2 %shard_map.78 = bf16[64,256,512]{2,1,0:T(8,128)(2,1)} custom-call(bf16[4,256,16,128]{3,2,1,0:T(8,128)(2,1)} %bitcast.48, bf16[64,128,128]{2,1,0:T(8,128)(2,1)} %bitcast.47, bf16[128,256]{1,0:T(8,128)(2,1)} %pad_maximum_fusion.1.x_back, bf16[256,448]{1,0:T(8,128)(2,1)} %pad_maximum_fusion.y_back, bf16[128,512]{1,0:T(8,128)(2,1)} %compare_convert_fusion.layer_mask, ...), custom_call_target="tpu_custom_call" | custom-call | tf_op jit(solution)/shard_map/pallas_call | solution.py:278
  (26 shorter events, 0.2 us)
Async XLA Ops:
  17.9 6.5 %copy-start.5 = (s32[128]{0:T(128)S(1)}, s32[128]{0:T(128)}, u32[]{:S(2)}) copy-start(s32[128]{0:T(128)} %tiles.1) | copy-start | bytes 1540
  17.9 54.7 %all-to-all-start = ((bf16[128,64,128]{2,1,0:T(8,128)(2,1)}), bf16[128,64,128]{2,1,0:T(8,128)(2,1)S(1)}, u32[]{:S(2)}, u32[]{:S(2)}) async-start(bf16[128,64,128]{2,1,0:T(8,128)(2,1)} %shard_map.73), calls=%async_computation | async-start | bytes 4194304 | tf_op jit(solution)/shard_map/all_to_all | solution.py:341
  24.3 150.7 %all-gather.5.cloned.1.call-start = ((), (), s32[]{:S(2)}) async-start(), calls=%async_computation.1 | async-start | bytes 5242880 | tf_op jit(solution)/shard_map/all_gather | solution.py:439
  72.6 1.3 copy-start
  81.5 9.9 %collective-permute-start = (bf16[16,256,128]{2,1,0:T(8,128)(2,1)}, bf16[16,256,128]{2,1,0:T(8,128)(2,1)S(1)}, u32[]{:S(2)}, u32[]{:S(2)}) collective-permute-start(bf16[16,256,128]{2,1,0:T(8,128)(2,1)} %shard_map.75), channel_id=1, source_target_pairs={{0,4},{4,0},{8,12},{12,8},{1,5},{5,1},{9,13},{13,9},{2,6},{6,2},{1... | collective-permute-start | bytes 3145736 | tf_op jit(solution)/shard_map/ppermute | solution.py:418
  92.9 25.6 %collective-permute-start.2 = (bf16[16,256,128]{2,1,0:T(8,128)(2,1)S(1)}, bf16[16,256,128]{2,1,0:T(8,128)(2,1)S(1)}, u32[]{:S(2)}, u32[]{:S(2)}) collective-permute-start(bf16[16,256,128]{2,1,0:T(8,128)(2,1)S(1)} %add_convert_fusion), channel_id=1, source_target_pairs={{0,8},{4,12},{8,0},{12,4},{1,9},{5,13},{9,1},{13,5},{2,10},{6,14},... | collective-permute-start | bytes 3145736 | tf_op jit(solution)/shard_map/ppermute | solution.py:437
  109.6 8.9 %collective-permute-start.1 = (bf16[16,256,128]{2,1,0:T(8,128)(2,1)S(1)}, bf16[16,256,128]{2,1,0:T(8,128)(2,1)S(1)}, u32[]{:S(2)}, u32[]{:S(2)}) collective-permute-start(bf16[16,256,128]{2,1,0:T(8,128)(2,1)S(1)} %get-tuple-element.15), channel_id=1, source_target_pairs={{0,4},{4,0},{8,12},{12,8},{1,5},{5,1},{9,13},{13,9},{2,6},{6,2},{1... | collective-permute-start | bytes 3145736 | tf_op jit(solution)/shard_map/ppermute | solution.py:418
  118.5 1.0 copy-start.2
  118.5 1.3 copy-start.3
  119.9 15.1 %copy-start.4 = (bf16[64,64]{1,0:T(8,128)(2,1)S(1)}, bf16[64,64]{1,0:T(8,128)(2,1)}, u32[]{:S(2)}) copy-start(bf16[64,64]{1,0:T(8,128)(2,1)} %param.12) | copy-start | bytes 24580
  135.0 4.4 %copy-start.1 = (bf16[128,64,128]{2,1,0:T(8,128)(2,1)S(1)}, bf16[128,64,128]{2,1,0:T(8,128)(2,1)}, u32[]{:S(2)}) copy-start(bf16[128,64,128]{2,1,0:T(8,128)(2,1)} %copy-done) | copy-start | bytes 6291460
Sparse Core Ops, SparseCore 0:
  135.1 39.9 all-gather.4
